TPU v7x, 32 devices: a whole 2x2x4 slice. The times are simulated.
32 devices in a mesh: groups: 2 (over y), ctx: 4 (over x, core), tp: 4 (over z).
Axes of the slice: x: 2, y: 2, z: 4, core: 2. Of those that a mesh axis runs over, the one named last changes fastest.
Arguments:
- question_hidden: bfloat16 [256, 8192], P(('groups', 'ctx')), parts along dimension 0, may hold values from -1800 to 1800
- recomp_hidden: bfloat16 [512, 8192], P(('groups', 'ctx')), parts along dimension 0, may hold values from -1800 to 1800
- norm_gain: bfloat16 [8192], replicated, may hold values from 0.099609375 to 1.8984375
- w_query: bfloat16 [8192, 8192], P('ctx', 'tp'), may hold values from -0.0625 to 0.0625
- w_keyval: bfloat16 [8192, 2, 1024], P('ctx', None, 'tp'), may hold values from -0.25 to 0.25
- pool_codes: bfloat16 [384, 2, 64, 1024], P(('groups', 'ctx'), None, None, 'tp'), parts along dimension 0, may hold values from -127 to 127
- pool_scales: bfloat16 [384, 2, 8], P(('groups', 'ctx'), None, 'tp'), parts along dimension 0, may hold values from 0.025 to 2
- block_owner: int32 [256, 1], P('groups'), parts along dimension 0, may hold values from 0 to 3; in each aligned block of 32 rows (0 to 31, 32 to 63, ...) at most 16 rows name the same one
- block_slot: int32 [256], P('groups'), parts along dimension 0, may hold values from 0 to 47
- recomp_pos: int32 [512], P('groups'), parts along dimension 0, may hold values from 0 to 8191, as said below
Outputs:
- attended: bfloat16 [256, 8192], P(('groups', 'ctx'), 'tp'), parts along dimension 0
- kv_cache: bfloat16 [2, 16384, 1024], P(None, ('groups', 'ctx'), 'tp'), parts along dimension 1
There are 2 independent parts, one for each index of `groups`. A program takes and returns all parts, laid end to end along the dimension named above; an argument that names none is the same for every part. Nothing has to cross between parts.
Inputs may be any that keep to these rules, and one draw needn't show every extreme that they name: Among the 32 context blocks of each index of ctx (rows of block_owner in aligned blocks), at most 16 name the same pool shard. `recomp_pos`: 256 distinct positions in no particular order; the first and the last context position are always listed.
All inputs are finite; a program needn't handle non-finite values.
Results may differ from a plain program's by a relative error of at most 0.018.
The roundings to bfloat16 on the way count: a program that leaves them out, or rounds other values in their place, can miss the bound.
Values may be sent and summed in bfloat16 or wider, within the bound.
A program may use at most 128 MiB of HBM per device.

v0:
```python
import jax
import jax.numpy as jnp
from jax import lax
from jax.sharding import PartitionSpec as P

HD = 128


norm_eps = 1e-05
neg_large = -1e30


def rms_rows(hidden, norm_gain):
    floats = hidden.astype(jnp.float32)
    factor = lax.rsqrt(jnp.mean(floats * floats, axis=-1, keepdims=True) + norm_eps)
    return (floats * factor * norm_gain.astype(jnp.float32)).astype(jnp.bfloat16)


def attend_block(running, queries, key_rows, val_rows, visible, score_scale):
    row_max, row_total, weighted = running
    scores = (
        jnp.einsum("thgd,nhd->htgn", queries, key_rows, preferred_element_type=jnp.float32)
        * score_scale
    )
    shown = visible[None, :, None, :]
    masked = jnp.where(shown, scores, neg_large)
    new_max = jnp.maximum(row_max, jnp.max(masked, axis=-1))
    weights = jnp.where(shown, jnp.exp(masked - new_max[..., None]), 0.0)
    row_total = jnp.sum(weights, axis=-1)
    weighted = jnp.einsum(
        "htgn,nhd->htgd", weights.astype(jnp.bfloat16), val_rows, preferred_element_type=jnp.float32
    )
    return (new_max, row_total, weighted)


def fold_keys(running, queries, token_index, key_rows, val_rows, key_rank, score_scale):
    visible = key_rank[None, :] <= token_index[:, None]
    return attend_block(running, queries, key_rows, val_rows, visible, score_scale)


def empty_state(kv_heads, token_count, group_size):
    return (
        jnp.full((kv_heads, token_count, group_size), neg_large, jnp.float32),
        jnp.zeros((kv_heads, token_count, group_size), jnp.float32),
        jnp.zeros((kv_heads, token_count, group_size, HD), jnp.float32),
    )


def body(
    question_hidden,
    recomp_hidden,
    norm_gain,
    w_query,
    w_keyval,
    pool_codes,
    pool_scales,
    block_owner,
    block_slot,
    recomp_pos,
):
    shards = lax.axis_size("ctx")
    own_index = lax.axis_index("ctx")
    q_rows = question_hidden.shape[0]
    r_rows = recomp_hidden.shape[0]
    row_count = q_rows + r_rows
    kv_width = w_keyval.shape[2]
    kv_heads = kv_width // HD
    q_width = w_query.shape[1]
    group_size = q_width // kv_width
    score_scale = HD ** (-0.5)
    normed = jnp.concatenate(
        [rms_rows(question_hidden, norm_gain), rms_rows(recomp_hidden, norm_gain)], axis=0
    )
    pieces = lax.all_to_all(normed, "ctx", split_axis=1, concat_axis=0, tiled=True)
    arranged = pieces.reshape(shards, row_count, pieces.shape[1])
    question_part = arranged[:, :q_rows, :].reshape(shards * q_rows, pieces.shape[1])
    block_rows = question_part
    query = lax.psum_scatter(
        jnp.dot(block_rows, w_query, preferred_element_type=jnp.float32),
        "ctx",
        scatter_dimension=0,
        tiled=True,
    ).astype(jnp.bfloat16)
    kv_weight = w_keyval.reshape(w_keyval.shape[0], 2 * kv_width)
    block_rows = pieces
    projected = (
        lax.psum_scatter(
            jnp.dot(block_rows, kv_weight, preferred_element_type=jnp.float32),
            "ctx",
            scatter_dimension=0,
            tiled=True,
        )
        .astype(jnp.bfloat16)
        .reshape(row_count, 2, kv_width)
    )
    question_kv = projected[:q_rows]
    recomp_kv = projected[q_rows:]
    owners = block_owner[:, 0].reshape(shards, -1)
    per_dev = owners.shape[1]
    slot_table = block_slot.reshape(shards, per_dev)
    capacity = max(2, 2 * per_dev // shards)
    positions = jnp.arange(per_dev)
    earlier_mask = positions[None, :] < positions[:, None]
    same_owner = owners[:, :, None] == owners[:, None, :]
    order_rank = jnp.sum((same_owner & earlier_mask[None]).astype(jnp.int32), axis=2)
    slot_ids = jnp.arange(capacity)
    chosen = (owners == own_index)[:, :, None] & (order_rank[:, :, None] == slot_ids[None, None, :])
    send_slot = jnp.sum(jnp.where(chosen, slot_table[:, :, None], 0), axis=1).reshape(-1)
    send_codes = jnp.take(pool_codes, send_slot, axis=0).reshape(
        (shards, capacity) + pool_codes.shape[1:]
    )
    send_scales = jnp.take(pool_scales, send_slot, axis=0).reshape(
        (shards, capacity) + pool_scales.shape[1:]
    )
    got_codes, got_scales = (
        lax.all_to_all(send_codes, "ctx", split_axis=0, concat_axis=0, tiled=True),
        lax.all_to_all(send_scales, "ctx", split_axis=0, concat_axis=0, tiled=True),
    )
    own_owner = lax.dynamic_index_in_dim(owners, own_index, 0, keepdims=False)
    own_rank = lax.dynamic_index_in_dim(order_rank, own_index, 0, keepdims=False)
    flat_index = own_owner * capacity + own_rank
    block_codes = jnp.take(
        got_codes.reshape((shards * capacity,) + pool_codes.shape[1:]), flat_index, axis=0
    )
    block_scales = jnp.take(
        got_scales.reshape((shards * capacity,) + pool_scales.shape[1:]), flat_index, axis=0
    )
    block_len = block_codes.shape[2]
    dequant = (
        block_codes.astype(jnp.float32).reshape(per_dev, 2, block_len, kv_heads, HD)
        * block_scales.astype(jnp.float32)[:, :, None, :, None]
    )
    ctx_dev = per_dev * block_len
    cached = jnp.transpose(
        dequant.astype(jnp.bfloat16).reshape(per_dev, 2, block_len, kv_width), (1, 0, 2, 3)
    ).reshape(2, ctx_dev, kv_width)
    all_recomp = lax.all_gather(recomp_kv, "ctx", axis=0, tiled=True)
    local_pos = recomp_pos - own_index * ctx_dev
    target = jnp.where((local_pos >= 0) & (local_pos < ctx_dev), local_pos, ctx_dev)
    kv_cache = cached.at[:, target, :].set(jnp.transpose(all_recomp, (1, 0, 2)), mode="drop")
    key_local = jnp.concatenate([kv_cache[0], question_kv[:, 0]], axis=0)
    val_local = jnp.concatenate([kv_cache[1], question_kv[:, 1]], axis=0)
    key_span = ctx_dev + q_rows
    every_query = lax.all_gather(query, "ctx", axis=0, tiled=True)
    total_tokens = every_query.shape[0]
    per_step = q_rows
    while (
        per_step * 2 <= total_tokens
        and total_tokens % (per_step * 2) == 0
        and (per_step * group_size < 512)
    ):
        per_step = per_step * 2
    block_count = total_tokens // per_step
    query_blocks = every_query.reshape(block_count, per_step, kv_heads, group_size, HD)
    key_offset = jnp.arange(key_span)
    local_rank = jnp.where(key_offset < ctx_dev, -1, own_index * q_rows + key_offset - ctx_dev)
    key_three = key_local.reshape(key_span, kv_heads, HD)
    val_three = val_local.reshape(key_span, kv_heads, HD)

    def one_block(packed):
        block_queries, first_token = packed
        token_index = first_token + jnp.arange(per_step)
        return fold_keys(
            empty_state(kv_heads, per_step, group_size),
            block_queries,
            token_index,
            key_three,
            val_three,
            local_rank,
            score_scale,
        )

    part_max, part_total, part_sums = lax.map(
        one_block, (query_blocks, jnp.arange(block_count) * per_step)
    )

    def by_token(value, trailing):
        return jnp.moveaxis(value, 1, 2).reshape(shards, q_rows, trailing)

    sent = (
        by_token(part_sums, q_width),
        by_token(part_max, kv_heads * group_size),
        by_token(part_total, kv_heads * group_size),
    )
    got_sums, got_max, got_total = (
        lax.all_to_all(sent[0], "ctx", split_axis=0, concat_axis=0, tiled=True),
        lax.all_to_all(sent[1], "ctx", split_axis=0, concat_axis=0, tiled=True),
        lax.all_to_all(sent[2], "ctx", split_axis=0, concat_axis=0, tiled=True),
    )
    best_max = jnp.max(got_max, axis=0)
    factor = jnp.exp(got_max - best_max[None])
    row_total = jnp.sum(got_total * factor, axis=0)
    weighted = jnp.sum(
        got_sums.reshape(shards, q_rows, kv_heads * group_size, HD) * factor[..., None], axis=0
    )
    attended = (weighted / row_total[..., None]).reshape(q_rows, q_width).astype(jnp.bfloat16)
    return (attended, kv_cache)


def solution(mesh):
    placed = (
        P(("groups", "ctx"), None),
        P(("groups", "ctx"), None),
        P(),
        P("ctx", "tp"),
        P("ctx", None, "tp"),
        P(("groups", "ctx"), None, None, "tp"),
        P(("groups", "ctx"), None, "tp"),
        P("groups", None),
        P("groups"),
        P("groups"),
    )
    return jax.shard_map(
        body,
        mesh=mesh,
        in_specs=placed,
        out_specs=(P(("groups", "ctx"), "tp"), P(None, ("groups", "ctx"), "tp")),
        check_vma=False,
    )
```

profile of v0, /device:TPU:0, one launch (start us, length us, event | category | flops | bytes accessed | tf_op | source)
XLA Modules:
  0.0 228.9 jit_solution(15619929386132747075)
XLA Ops:
  12.7 4.2 %all-to-all-start.2 = ((bf16[4,16,2,2]{1,3,2,0:T(2,128)(2,1)}), bf16[4,16,2,2]{1,3,2,0:T(2,128)(2,1)S(1)}, u32[]{:S(2)}, u32[]{:S(2)}) async-start(bf16[4,16,2,2]{1,3,2,0:T(2,128)(2,1)} %broadcast_select_fusion.2), calls=%async_computation.3 | async-start | bytes 8192 | tf_op jit(solution)/shard_map/all_to_all | solution.py:117
  22.4 4.4 %all-to-all-start = ((bf16[96,4,2048]{2,0,1:T(8,128)(2,1)}), bf16[96,4,2048]{2,0,1:T(8,128)(2,1)}, u32[]{:S(2)}, u32[]{:S(2)}) async-start(bf16[96,4,2048]{2,0,1:T(8,128)(2,1)} %bitcast.108), calls=%async_computation | async-start | bytes 3145728 | tf_op jit(solution)/shard_map/all_to_all | solution.py:74
  26.8 2.8 %gather_fusion = bf16[64,2,64,256]{3,2,1,0:T(8,128)(2,1)} fusion(bf16[48,2,64,256]{3,2,1,0:T(8,128)(2,1)S(1)} %copy-done, s32[1024]{0:T(1024)S(1)} %pad_clamp_fusion.1), kind=kCustom, calls=%fused_computation | custom fusion | bytes 8388864 | tf_op jit(solution)/shard_map/jit(_take)/gather | solution.py:109
  29.6 4.6 %broadcast_select_fusion = bf16[4,16,2,64,256]{4,3,2,1,0:T(8,128)(2,1)} fusion(bf16[4,16,2,64,256]{4,3,2,1,0:T(8,128)(2,1)} %bitcast.105, pred[4,16]{1,0:T(4,128)(4,1)S(1)} %compare_and_fusion), kind=kLoop, calls=%fused_computation.32 | loop fusion | flops 2097152 | bytes 8388672 | tf_op jit(solution)/shard_map/jit(_take)/select_n | solution.py:109
  34.2 12.8 %all-to-all-done = bf16[96,4,2048]{2,0,1:T(8,128)(2,1)} async-done(((bf16[96,4,2048]{2,0,1:T(8,128)(2,1)}), bf16[96,4,2048]{2,0,1:T(8,128)(2,1)}, u32[]{:S(2)}, u32[]{:S(2)}) %all-to-all-start) | async-done | bytes 1572896 | tf_op jit(solution)/shard_map/all_to_all | solution.py:74
  47.0 4.8 %all-to-all-start.1 = ((bf16[4,16,2,64,256]{4,3,2,1,0:T(8,128)(2,1)}), bf16[4,16,2,64,256]{4,3,2,1,0:T(8,128)(2,1)}, u32[]{:S(2)}, u32[]{:S(2)}) async-start(bf16[4,16,2,64,256]{4,3,2,1,0:T(8,128)(2,1)} %broadcast_select_fusion), calls=%async_computation.2 | async-start | bytes 8388608 | tf_op jit(solution)/shard_map/all_to_all | solution.py:116
  52.4 3.3 %fusion.35 = f32[384,512]{1,0:T(8,128)} fusion(bf16[384,2048]{1,0:T(8,128)(2,1)} %bitcast.13, bf16[2048,512]{1,0:T(8,128)(2,1)S(1)} %bitcast.115), kind=kOutput, calls=%fused_computation.83 | convolution fusion | flops 805306368 | bytes 4456448 | tf_op jit(solution)/shard_map/dot_general | solution.py:88
  59.1 5.7 %fusion.34 = f32[128,2048]{1,0:T(8,128)} fusion(bf16[128,2048]{1,0:T(8,128)(2,1)S(1)} %bitcast.112, bf16[2048,2048]{1,0:T(8,128)(2,1)} %param.15), kind=kOutput, calls=%fused_computation.82 | convolution fusion | flops 1073741824 | bytes 9961472 | tf_op jit(solution)/shard_map/dot_general | solution.py:79
  64.9 20.8 %reduce-scatter.5.cloned.1.call-done = f32[96,512]{1,0:T(8,128)} async-done(((f32[384,512]{1,0:T(8,128)}), f32[96,512]{1,0:T(8,128)}) %reduce-scatter.5.cloned.1.call-update) | async-done | bytes 196624 | tf_op jit(solution)/shard_map/reduce_scatter | solution.py:87
  87.0 19.4 %all_gather.7 = bf16[256,2,256]{2,1,0:T(2,128)(2,1)S(1)} all-gather(bf16[64,2,256]{2,1,0:T(2,128)(2,1)S(1)} %slice.29), channel_id=1, replica_groups=mesh['groups'=2,'ctx'=4,'tp'=4] {'ctx'}, dimensions={0}, use_global_device_ids=true | all-gather | bytes 327680 | tf_op jit(solution)/shard_map/all_gather | solution.py:137
  106.4 2.9 %gather_fusion.1 = bf16[32,2,64,256]{3,2,1,0:T(8,128)(2,1)S(1)} fusion(bf16[64,2,64,256]{3,2,1,0:T(8,128)(2,1)} %bitcast.5, s32[1024]{0:T(1024)S(1)} %pad_clamp_fusion), kind=kCustom, calls=%fused_computation.1 | custom fusion | bytes 4194432 | tf_op jit(solution)/shard_map/jit(_take)/gather | solution.py:122
  110.6 12.8 %copy.83 = bf16[2,2048,256]{2,0,1:T(2,128)(2,1)S(1)} copy(bf16[2,2048,256]{2,1,0:T(8,128)(2,1)S(1)} %bitcast.106) | data formatting | bytes 4194304 | tf_op jit(solution)/shard_map/reshape | solution.py:136
  123.4 7.5 %scatter_fusion = bf16[2,2048,256]{2,0,1:T(2,128)(2,1)S(1)} fusion(bf16[2,2048,256]{2,0,1:T(2,128)(2,1)S(1)} %copy.83, s32[256]{0:T(256)S(1)} %copy-done.10, bf16[256,2,256]{2,1,0:T(2,128)(2,1)S(1)} %all_gather.7), kind=kCustom, calls=%fused_computation.4 | custom fusion | bytes 787456 | tf_op jit(solution)/shard_map/scatter | solution.py:140
  130.9 4.2 %fusion.32 = (bf16[1,2048,256]{2,0,1:T(2,128)(2,1)}, bf16[1,2048,256]{2,0,1:T(2,128)(2,1)}) fusion(bf16[2,2048,256]{2,0,1:T(2,128)(2,1)S(1)} %scatter_fusion), kind=kLoop, calls=%fused_computation.77 | loop fusion | bytes 4194304 | tf_op jit(solution)/shard_map/slice | solution.py:142
  135.0 4.6 %copy.84 = bf16[1,2048,256]{1,2,0:T(8,128)(2,1)S(1)} copy(bf16[1,2048,256]{2,0,1:T(2,128)(2,1)} %get-tuple-element.157) | data formatting | bytes 2097152 | tf_op jit(solution)/shard_map/slice | solution.py:141
  142.3 5.9 %copy.87 = bf16[1,2048,256]{1,2,0:T(8,128)(2,1)} copy(bf16[1,2048,256]{2,0,1:T(2,128)(2,1)} %get-tuple-element.156) | data formatting | bytes 2097152 | tf_op jit(solution)/shard_map/slice | solution.py:142
  148.2 2.3 %pad_maximum_fusion.2 = bf16[2080,2,128]{0,2,1:T(8,128)(2,1)} fusion(bf16[32,2,128]{0,2,1:T(8,128)(2,1)S(1)} %bitcast.119, bf16[2048,2,128]{0,2,1:T(8,128)(2,1)} %bitcast.111), kind=kLoop, calls=%fused_computation.43 | loop fusion | flops 2129920 | bytes 2129920 | tf_op jit(solution)/shard_map/concatenate | solution.py:142
  150.5 2.3 %copy.92 = bf16[2080,2,128]{2,0,1:T(8,128)(2,1)} copy(bf16[2080,2,128]{0,2,1:T(8,128)(2,1)} %pad_maximum_fusion.2) | data formatting | bytes 2129920
  153.8 7.5 %all_gather.6 = bf16[128,2048]{1,0:T(8,128)(2,1)S(1)} all-gather(bf16[32,2048]{1,0:T(8,128)(2,1)S(1)} %convert_element_type.57), channel_id=1, replica_groups=mesh['groups'=2,'ctx'=4,'tp'=4] {'ctx'}, dimensions={0}, use_global_device_ids=true | all-gather | bytes 655360 | tf_op jit(solution)/shard_map/all_gather | solution.py:144
  162.2 23.5 %while.15 = (s32[]{:T(128)}, f32[2,2,64,8]{3,2,1,0:T(8,128)S(1)}, f32[2,2,64,8]{3,2,1,0:T(8,128)S(1)}, f32[2,2,64,8,128]{4,3,2,1,0:T(8,128)}, s32[2]{0:T(128)S(1...) while((s32[]{:T(128)}, f32[2,2,64,8]{3,2,1,0:T(8,128)S(1)}, ...), condition=%wide.region_10.11_spmd.clone, body=%wide.region_7.10_spmd.clone.sunk | while | flops 1118349568 | bytes 42421216 | solution.py:173
  163.6 3.4 %fusion.47 = (f32[2,64,8]{2,1,0:T(8,128)S(1)}, f32[2,64,8,2080]{3,2,1,0:T(8,128)S(1)}) fusion(pred[64,2080]{1,0:T(8,128)(4,1)S(1)} %broadcast_compare_fusion.3, bf16[2080,2,128]{2,0,1:T(8,128)(2,1)S(1)} %get-tuple-element.249, bf16[2,64,2,8,128]{4,3,2,1,0:T(8,128)(2,1)} %get-tuple-element.248, s32[]{:T(128)S(6)} %copy.137), kind=kOutput, calls=%fused_computation.8.clone.1 | convolution fusion | flops 551648256 | bytes 9984004 | tf_op jit(solution)/shard_map/while/body/eval_jaxpr/thgd,nhd->htgn/dot_general | solution.py:22
  167.1 3.2 %fusion.48 = f32[2,64,8]{2,1,0:T(8,128)S(1)} fusion(f32[2,64,8,2080]{3,2,1,0:T(8,128)S(1)} %get-tuple-element.219, f32[2,64,8]{2,1,0:T(8,128)S(1)} %broadcast_maximum_fusion.2, pred[64,2080]{1,0:T(8,128)(4,1)S(1)} %broadcast_compare_fusion.3), kind=kLoop, calls=%fused_computation.10.clone.1 | loop fusion | flops 10648576 | bytes 8660992 | tf_op jit(solution)/shard_map/while/body/eval_jaxpr/reduce_sum | solution.py:29
  170.4 2.6 %fusion.49 = f32[2,2,64,8,128]{4,3,2,1,0:T(8,128)S(1)} fusion(f32[2,2,64,8,128]{4,3,2,1,0:T(8,128)S(1)} %copy-done.6, s32[]{:T(128)S(6)} %copy.137, f32[2,64,8,2080]{3,2,1,0:T(8,128)S(1)} %get-tuple-element.219, f32[2,64,8]{2,1,0:T(8,128)S(1)} %broadcast_maximum_fusion.2, pred[64,2080]{1,0:T(8,128)(4,1)S(1)} %broadcast_compare_fusion.3, ...), kind=kOutput, calls=%fused_computation.14.clone.1 | convolution fusion | flops 555909120 | bytes 10706948 | tf_op jit(solution)/shard_map/while/body/eval_jaxpr/htgn,nhd->htgd/dot_general | solution.py:30
  175.4 3.4 %fusion.47 = (f32[2,64,8]{2,1,0:T(8,128)S(1)}, f32[2,64,8,2080]{3,2,1,0:T(8,128)S(1)}) fusion(pred[64,2080]{1,0:T(8,128)(4,1)S(1)} %broadcast_compare_fusion.3, bf16[2080,2,128]{2,0,1:T(8,128)(2,1)S(1)} %get-tuple-element.249, bf16[2,64,2,8,128]{4,3,2,1,0:T(8,128)(2,1)} %get-tuple-element.248, s32[]{:T(128)S(6)} %copy.137), kind=kOutput, calls=%fused_computation.8.clone.1 | convolution fusion | flops 551648256 | bytes 9984004 | tf_op jit(solution)/shard_map/while/body/eval_jaxpr/thgd,nhd->htgn/dot_general | solution.py:22
  178.9 3.2 %fusion.48 = f32[2,64,8]{2,1,0:T(8,128)S(1)} fusion(f32[2,64,8,2080]{3,2,1,0:T(8,128)S(1)} %get-tuple-element.219, f32[2,64,8]{2,1,0:T(8,128)S(1)} %broadcast_maximum_fusion.2, pred[64,2080]{1,0:T(8,128)(4,1)S(1)} %broadcast_compare_fusion.3), kind=kLoop, calls=%fused_computation.10.clone.1 | loop fusion | flops 10648576 | bytes 8660992 | tf_op jit(solution)/shard_map/while/body/eval_jaxpr/reduce_sum | solution.py:29
  182.1 2.6 %fusion.49 = f32[2,2,64,8,128]{4,3,2,1,0:T(8,128)S(1)} fusion(f32[2,2,64,8,128]{4,3,2,1,0:T(8,128)S(1)} %copy-done.6, s32[]{:T(128)S(6)} %copy.137, f32[2,64,8,2080]{3,2,1,0:T(8,128)S(1)} %get-tuple-element.219, f32[2,64,8]{2,1,0:T(8,128)S(1)} %broadcast_maximum_fusion.2, pred[64,2080]{1,0:T(8,128)(4,1)S(1)} %broadcast_compare_fusion.3, ...), kind=kOutput, calls=%fused_computation.14.clone.1 | convolution fusion | flops 555909120 | bytes 10706948 | tf_op jit(solution)/shard_map/while/body/eval_jaxpr/htgn,nhd->htgd/dot_general | solution.py:30
  186.6 3.2 %all-to-all-start.4 = ((f32[4,1,512]{2,1,0:T(1,128)}), f32[4,1,512]{2,1,0:T(1,128)S(1)}, u32[]{:S(2)}, u32[]{:S(2)}) async-start(f32[4,1,512]{2,1,0:T(1,128)} %reshape.295), calls=%async_computation.6 | async-start | bytes 16384 | tf_op jit(solution)/shard_map/all_to_all | solution.py:187
  190.8 2.9 %all-to-all-done.4 = f32[4,1,512]{2,1,0:T(1,128)S(1)} async-done(((f32[4,1,512]{2,1,0:T(1,128)}), f32[4,1,512]{2,1,0:T(1,128)S(1)}, u32[]{:S(2)}, u32[]{:S(2)}) %all-to-all-start.4) | async-done | bytes 8224 | tf_op jit(solution)/shard_map/all_to_all | solution.py:187
  193.7 3.2 %all-to-all-start.5 = ((f32[4,1,512]{2,1,0:T(1,128)}), f32[4,1,512]{2,1,0:T(1,128)S(1)}, u32[]{:S(2)}, u32[]{:S(2)}) async-start(f32[4,1,512]{2,1,0:T(1,128)} %reshape.297), calls=%async_computation.7 | async-start | bytes 16384 | tf_op jit(solution)/shard_map/all_to_all | solution.py:188
  200.7 4.2 %all-to-all-start.3 = ((f32[4,32,2048]{2,1,0:T(8,128)}), f32[4,32,2048]{2,1,0:T(8,128)}, u32[]{:S(2)}, u32[]{:S(2)}) async-start(f32[4,32,2048]{2,1,0:T(8,128)} %reshape.240), calls=%async_computation.5 | async-start | bytes 2097152 | tf_op jit(solution)/shard_map/all_to_all | solution.py:186
  210.0 2.4 %mul.118 = f32[4,32,2048]{2,1,0:T(8,128)} reshape(f32[4,32,16,128]{3,2,1,0:T(8,128)} %mul.117) | data formatting | bytes 2097152 | tf_op jit(solution)/shard_map/mul | solution.py:194
  212.5 7.0 %all-to-all-done.3 = f32[4,32,2048]{2,1,0:T(8,128)} async-done(((f32[4,32,2048]{2,1,0:T(8,128)}), f32[4,32,2048]{2,1,0:T(8,128)}, u32[]{:S(2)}, u32[]{:S(2)}) %all-to-all-start.3) | async-done | bytes 1048608 | tf_op jit(solution)/shard_map/all_to_all | solution.py:186
  (130 shorter events, 40.0 us)
Async XLA Ops:
  7.2 19.7 %copy-start = (bf16[48,2,64,256]{3,2,1,0:T(8,128)(2,1)S(1)}, bf16[48,2,64,256]{3,2,1,0:T(8,128)(2,1)}, u32[]{:S(2)}) copy-start(bf16[48,2,64,256]{3,2,1,0:T(8,128)(2,1)} %param.17) | copy-start | bytes 9437188
  12.7 9.8 %all-to-all-start.2 = ((bf16[4,16,2,2]{1,3,2,0:T(2,128)(2,1)}), bf16[4,16,2,2]{1,3,2,0:T(2,128)(2,1)S(1)}, u32[]{:S(2)}, u32[]{:S(2)}) async-start(bf16[4,16,2,2]{1,3,2,0:T(2,128)(2,1)} %broadcast_select_fusion.2), calls=%async_computation.3 | async-start | bytes 8192 | tf_op jit(solution)/shard_map/all_to_all | solution.py:117
  16.9 3.7 %copy-start.2 = (bf16[64,8192]{1,0:T(8,128)(2,1)S(1)}, bf16[64,8192]{1,0:T(8,128)(2,1)}, u32[]{:S(2)}) copy-start(bf16[64,8192]{1,0:T(8,128)(2,1)} %param.13) | copy-start | bytes 3145732
  16.9 4.0 %copy-start.4 = (bf16[32,8192]{1,0:T(8,128)(2,1)S(1)}, bf16[32,8192]{1,0:T(8,128)(2,1)}, u32[]{:S(2)}) copy-start(bf16[32,8192]{1,0:T(8,128)(2,1)} %param.12) | copy-start | bytes 1572868
  22.4 24.5 %all-to-all-start = ((bf16[96,4,2048]{2,0,1:T(8,128)(2,1)}), bf16[96,4,2048]{2,0,1:T(8,128)(2,1)}, u32[]{:S(2)}, u32[]{:S(2)}) async-start(bf16[96,4,2048]{2,0,1:T(8,128)(2,1)} %bitcast.108), calls=%async_computation | async-start | bytes 3145728 | tf_op jit(solution)/shard_map/all_to_all | solution.py:74
  34.2 17.7 %copy-start.3 = (bf16[2048,2,256]{2,1,0:T(2,128)(2,1)S(1)}, bf16[2048,2,256]{2,1,0:T(2,128)(2,1)}, u32[]{:S(2)}) copy-start(bf16[2048,2,256]{2,1,0:T(2,128)(2,1)} %param.16) | copy-start | bytes 6291460
  47.0 59.4 %all-to-all-start.1 = ((bf16[4,16,2,64,256]{4,3,2,1,0:T(8,128)(2,1)}), bf16[4,16,2,64,256]{4,3,2,1,0:T(8,128)(2,1)}, u32[]{:S(2)}, u32[]{:S(2)}) async-start(bf16[4,16,2,64,256]{4,3,2,1,0:T(8,128)(2,1)} %broadcast_select_fusion), calls=%async_computation.2 | async-start | bytes 8388608 | tf_op jit(solution)/shard_map/all_to_all | solution.py:116
  51.8 33.8 %reduce-scatter.5.cloned.1.call-start = ((), (), s32[]{:S(2)}) async-start(), calls=%async_computation.9 | async-start | bytes 983040 | tf_op jit(solution)/shard_map/reduce_scatter | solution.py:87
  52.3 4.0 %copy-start.11 = (s32[256]{0:T(256)S(1)}, s32[256]{0:T(256)}, u32[]{:S(2)}) copy-start(s32[256]{0:T(256)} %param.21) | copy-start | bytes 3076
  55.7 97.2 %reduce-scatter.3.cloned.1.call-start = ((), (), s32[]{:S(2)}) async-start(), calls=%async_computation.8 | async-start | bytes 1310720 | tf_op jit(solution)/shard_map/reduce_scatter | solution.py:78
  110.6 12.8 %copy-start.10 = (s32[256]{0:T(256)S(1)}, s32[256]{0:T(256)}, u32[]{:S(2)}) copy-start(s32[256]{0:T(256)} %compare_select_fusion.1) | copy-start | bytes 3076
  150.5 11.7 %copy-start.8 = (f32[2,2,64,8]{3,2,1,0:T(8,128)S(1)}, f32[2,2,64,8]{3,2,1,0:T(8,128)}, u32[]{:S(2)}) copy-start(f32[2,2,64,8]{3,2,1,0:T(8,128)} %custom-call.8) | copy-start | bytes 24580
  150.5 11.7 %copy-start.9 = (f32[2,2,64,8]{3,2,1,0:T(8,128)S(1)}, f32[2,2,64,8]{3,2,1,0:T(8,128)}, u32[]{:S(2)}) copy-start(f32[2,2,64,8]{3,2,1,0:T(8,128)} %custom-call.9) | copy-start | bytes 24580
  150.5 11.7 %copy-start.12 = (s32[2]{0:T(128)S(1)}, s32[2]{0:T(128)}, u32[]{:S(2)}) copy-start(s32[2]{0:T(128)} %iota_multiply_fusion) | copy-start | bytes 28
  167.1 3.3 %copy-start.5 = (bf16[2080,2,128]{2,0,1:T(8,128)(2,1)S(1)}, bf16[2080,2,128]{2,0,1:T(8,128)(2,1)}, u32[]{:S(2)}) copy-start(bf16[2080,2,128]{2,0,1:T(8,128)(2,1)} %get-tuple-element.250) | copy-start | bytes 3194884 | tf_op jit(solution)/shard_map/while
  167.1 3.3 %copy-start.6 = (f32[2,2,64,8,128]{4,3,2,1,0:T(8,128)S(1)}, f32[2,2,64,8,128]{4,3,2,1,0:T(8,128)}, u32[]{:S(2)}) copy-start(f32[2,2,64,8,128]{4,3,2,1,0:T(8,128)} %get-tuple-element.236) | copy-start | bytes 3145732 | tf_op jit(solution)/shard_map/while
  173.0 1.0 copy-start.7
  178.8 3.3 %copy-start.5 = (bf16[2080,2,128]{2,0,1:T(8,128)(2,1)S(1)}, bf16[2080,2,128]{2,0,1:T(8,128)(2,1)}, u32[]{:S(2)}) copy-start(bf16[2080,2,128]{2,0,1:T(8,128)(2,1)} %get-tuple-element.250) | copy-start | bytes 3194884 | tf_op jit(solution)/shard_map/while
  178.9 3.3 %copy-start.6 = (f32[2,2,64,8,128]{4,3,2,1,0:T(8,128)S(1)}, f32[2,2,64,8,128]{4,3,2,1,0:T(8,128)}, u32[]{:S(2)}) copy-start(f32[2,2,64,8,128]{4,3,2,1,0:T(8,128)} %get-tuple-element.236) | copy-start | bytes 3145732 | tf_op jit(solution)/shard_map/while
  184.7 1.0 copy-start.7
  186.6 7.0 %all-to-all-start.4 = ((f32[4,1,512]{2,1,0:T(1,128)}), f32[4,1,512]{2,1,0:T(1,128)S(1)}, u32[]{:S(2)}, u32[]{:S(2)}) async-start(f32[4,1,512]{2,1,0:T(1,128)} %reshape.295), calls=%async_computation.6 | async-start | bytes 16384 | tf_op jit(solution)/shard_map/all_to_all | solution.py:187
  193.7 7.0 %all-to-all-start.5 = ((f32[4,1,512]{2,1,0:T(1,128)}), f32[4,1,512]{2,1,0:T(1,128)S(1)}, u32[]{:S(2)}, u32[]{:S(2)}) async-start(f32[4,1,512]{2,1,0:T(1,128)} %reshape.297), calls=%async_computation.7 | async-start | bytes 16384 | tf_op jit(solution)/shard_map/all_to_all | solution.py:188
  200.7 18.8 %all-to-all-start.3 = ((f32[4,32,2048]{2,1,0:T(8,128)}), f32[4,32,2048]{2,1,0:T(8,128)}, u32[]{:S(2)}, u32[]{:S(2)}) async-start(f32[4,32,2048]{2,1,0:T(8,128)} %reshape.240), calls=%async_computation.5 | async-start | bytes 2097152 | tf_op jit(solution)/shard_map/all_to_all | solution.py:186
  208.7 13.4 %copy-start.1 = (bf16[48,2,64,256]{3,2,1,0:T(8,128)(2,1)S(1)}, bf16[48,2,64,256]{3,2,1,0:T(8,128)(2,1)}, u32[]{:S(2)}) copy-start(bf16[48,2,64,256]{3,2,1,0:T(8,128)(2,1)} %param.17) | copy-start | bytes 9437188
Sparse Core Ops, SparseCore 0:
  55.8 29.8 reduce-scatter.4
  88.3 24.9 reduce-scatter.2
where the time goes:
time: 230 us; the launch traced here: 229 us
  local copies, waits for them, and re-layouts  66.5 us (29%)
  waiting for transfers between devices  44.8 us (19%)
  other arithmetic  30.7 us (13%)
  blocking collectives  26.9 us (12%)
  starting transfers between devices  24.3 us (11%)
  matrix products  21 us (9%)
  between operations  14.5 us (6%)
    reduce_scatter x1, waiting for transfers between devices, body(): lax.psum_scatter(jnp.dot(block_rows, kv_weight, preferred_element_type=jn...  20.8 us
    all_gather x1, blocking collectives, body(): all_recomp = lax.all_gather(recomp_kv, 'ctx', axis=0, tiled=True)  19.4 us
    reshape x1, local copies, waits for them, and re-layouts, body(): cached = jnp.transpose(dequant.astype(jnp.bfloat16).reshape(per_dev, 2, b...  12.8 us
    all_to_all x1, waiting for transfers between devices, body(): lax.all_to_all(normed, 'ctx', split_axis=1, concat_axis=0, tiled=True)  12.8 us
    slice x3, local copies, waits for them, and re-layouts, body(): val_local = jnp.concatenate([kv_cache[1], question_kv[:, 1]], axis=0)  10.1 us
    unnamed x31, local copies, waits for them, and re-layouts  9.79 us
    all_gather x1, blocking collectives, body(): every_query = lax.all_gather(query, 'ctx', axis=0, tiled=True)  7.51 us
    scatter x1, local copies, waits for them, and re-layouts, body(): cached.at[:, target, :]  7.47 us
  transfers between devices with their start and end apart: 8, of which 5 were waited for; matrix products, arithmetic and copies ran while one was open for 37% of the time, Pallas kernels for 0%

commit v1 on v0

v1 whole, which is shorter than its diff:
```python
import functools
import math

import jax
import jax.numpy as jnp
from jax import lax
from jax.experimental import pallas as pl
from jax.experimental.pallas import tpu as pltpu
from jax.sharding import PartitionSpec as P

HD = 128
norm_eps = 1e-05
LANES = 128
VMEM = pltpu.VMEM
SMEM = pltpu.SMEM


def rms_rows(hidden, norm_gain):
    floats = hidden.astype(jnp.float32)
    factor = lax.rsqrt(jnp.mean(floats * floats, axis=-1, keepdims=True) + norm_eps)
    return (floats * factor * norm_gain.astype(jnp.float32)).astype(jnp.bfloat16)


def pick_kernel(per_dev, owner_ref, slot_ref, pool_ref, send_ref, sem):
    me = lax.axis_index("ctx")
    total_blocks = owner_ref.shape[0]

    def step(b, carry):
        count, total = carry
        dest = b // per_dev
        count = jnp.where(b % per_dev == 0, 0, count)
        mine = (owner_ref[b] == me) & (dest != me)

        @pl.when(mine)
        def _():
            pltpu.make_async_copy(
                pool_ref.at[slot_ref[b]], send_ref.at[dest, count], sem
            ).start()

        more = jnp.where(mine, 1, 0)
        return count + more, total + more

    _, total = lax.fori_loop(0, total_blocks, step, (jnp.int32(0), jnp.int32(0)))

    def drain(_, carry):
        pltpu.make_async_copy(pool_ref.at[0], send_ref.at[0, 0], sem).wait()
        return carry

    lax.fori_loop(0, total, drain, 0)


def pick_blocks(owner, slot, pool_codes, shards, capacity):
    per_dev = owner.shape[0] // shards
    return pl.pallas_call(
        functools.partial(pick_kernel, per_dev),
        out_shape=jax.ShapeDtypeStruct((shards, capacity) + pool_codes.shape[1:], pool_codes.dtype),
        in_specs=[
            pl.BlockSpec(memory_space=SMEM),
            pl.BlockSpec(memory_space=SMEM),
            pl.BlockSpec(memory_space=pl.ANY),
        ],
        out_specs=pl.BlockSpec(memory_space=pl.ANY),
        scratch_shapes=[pltpu.SemaphoreType.DMA],
        name="pick_blocks",
    )(owner, slot, pool_codes)


def attend_kernel(
    per_dev,
    kv_heads,
    owner_ref,
    slot_ref,
    scale_ref,
    pool_ref,
    codes_ref,
    query_ref,
    recomp_ref,
    own_kv_ref,
    pos_ref,
    sums_ref,
    lse_ref,
    cache_ref,
    raw,
    kv,
    tally,
    in_sem,
    out_sem,
):
    me = lax.axis_index("ctx")
    shards = codes_ref.shape[0]
    pool_dev = pool_ref.shape[0]
    block_len = pool_ref.shape[2]
    kv_width = kv_heads * HD
    tokens, q_width = query_ref.shape
    q_rows = own_kv_ref.shape[0]
    recomps = recomp_ref.shape[0]
    ctx_dev = per_dev * block_len
    group = q_width // kv_width
    base = me * per_dev

    for s in range(shards):
        tally[s] = 0

    def begin(b, carry):
        owner = owner_ref[base + b]
        rank = tally[owner]
        tally[owner] = rank + 1

        @pl.when(owner == me)
        def _():
            pltpu.make_async_copy(
                pool_ref.at[slot_ref[base + b]], raw.at[b], in_sem.at[b]
            ).start()

        @pl.when(owner != me)
        def _():
            pltpu.make_async_copy(codes_ref.at[owner, rank], raw.at[b], in_sem.at[b]).start()

        return carry

    lax.fori_loop(0, per_dev, begin, 0)

    per_chunk = math.gcd(8, per_dev)
    chunk = per_chunk * block_len

    def fill(i, carry):
        start = pl.multiple_of(i * chunk, chunk)
        local = pos_ref[...] - (me * ctx_dev + start)
        spot = lax.broadcasted_iota(jnp.int32, (chunk, recomps), 0)
        hit = jnp.where(spot == local, 1.0, 0.0).astype(jnp.float32)
        given = jnp.max(hit, axis=1, keepdims=True)
        blended = jnp.dot(
            hit.astype(jnp.bfloat16), recomp_ref[...], preferred_element_type=jnp.float32
        )
        for k in range(per_chunk):
            b = i * per_chunk + k
            pltpu.make_async_copy(pool_ref.at[0], raw.at[b], in_sem.at[b]).wait()
            at = (owner_ref[base + b] * pool_dev + slot_ref[base + b]) * (2 * kv_heads)
            rows = slice(k * block_len, (k + 1) * block_len)
            shown = given[rows] > 0.5
            for c in range(2):
                for h in range(kv_heads):
                    lanes = slice(h * HD, (h + 1) * HD)
                    wide = slice(c * kv_width + h * HD, c * kv_width + (h + 1) * HD)
                    value = raw[b, c, :, lanes].astype(jnp.float32) * scale_ref[at + c * kv_heads + h]
                    value = jnp.where(shown, blended[rows, wide], value)
                    kv[c, pl.ds(start + k * block_len, block_len), lanes] = value.astype(jnp.bfloat16)
        for c in range(2):
            pltpu.make_async_copy(
                kv.at[c, pl.ds(start, chunk)], cache_ref.at[c, pl.ds(start, chunk)], out_sem.at[i, c]
            ).start()
        return carry

    lax.fori_loop(0, per_dev // per_chunk, fill, 0)

    heads_step = math.gcd(group, max(1, 512 // tokens))
    rows = heads_step * tokens
    factor = HD ** (-0.5) * math.log2(math.e)
    lse_ref[...] = jnp.zeros_like(lse_ref)
    contract = (((1,), (1,)), ((), ()))
    lane = lax.broadcasted_iota(jnp.int32, (tokens, LANES), 1)
    row = lax.broadcasted_iota(jnp.int32, (rows, q_rows), 0)
    col = lax.broadcasted_iota(jnp.int32, (rows, q_rows), 1)
    visible = col + me * q_rows <= lax.rem(row, tokens)

    for h in range(kv_heads):
        lanes = slice(h * HD, (h + 1) * HD)
        vals = slice(kv_width + h * HD, kv_width + (h + 1) * HD)

        def one(i, carry):
            first = h * group + i * heads_step
            parts = [
                query_ref[:, pl.ds(pl.multiple_of((first + j) * HD, HD), HD)] for j in range(heads_step)
            ]
            q = parts[0] if heads_step == 1 else jnp.concatenate(parts, axis=0)
            s = lax.dot_general(q, kv[0, :, lanes], contract, preferred_element_type=jnp.float32)
            t = lax.dot_general(q, own_kv_ref[:, lanes], contract, preferred_element_type=jnp.float32)
            t = jnp.where(visible, t, -1e30)
            top = jnp.maximum(jnp.max(s, axis=1, keepdims=True), jnp.max(t, axis=1, keepdims=True))
            ps = jnp.exp2((s - top) * factor)
            pt = jnp.where(visible, jnp.exp2((t - top) * factor), 0.0)
            total = jnp.sum(ps, axis=1, keepdims=True) + jnp.sum(pt, axis=1, keepdims=True)
            o = jnp.dot(ps.astype(jnp.bfloat16), kv[1, :, lanes], preferred_element_type=jnp.float32)
            o = o + jnp.dot(
                pt.astype(jnp.bfloat16), own_kv_ref[:, vals], preferred_element_type=jnp.float32
            )
            o = o / total
            lse = top * factor + jnp.log2(total)
            for j in range(heads_step):
                here = slice(j * tokens, (j + 1) * tokens)
                sums_ref[:, pl.ds(pl.multiple_of((first + j) * HD, HD), HD)] = o[here].astype(
                    jnp.bfloat16
                )
                lse_ref[...] = jnp.where(lane == first + j, lse[here], lse_ref[...])
            return carry

        lax.fori_loop(0, group // heads_step, one, 0)

    def finish(i, carry):
        for c in range(2):
            pltpu.make_async_copy(
                kv.at[c, pl.ds(0, chunk)], cache_ref.at[c, pl.ds(0, chunk)], out_sem.at[i, c]
            ).wait()
        return carry

    lax.fori_loop(0, per_dev // per_chunk, finish, 0)


def attend(owner, slot, scales, pool_codes, got_codes, query, recomp_kv, own_kv, positions):
    shards = got_codes.shape[0]
    per_dev = owner.shape[0] // shards
    block_len, kv_width = pool_codes.shape[2:]
    tokens, q_width = query.shape
    ctx_dev = per_dev * block_len
    per_chunk = math.gcd(8, per_dev)
    smem, vmem, hbm = (pl.BlockSpec(memory_space=m) for m in (SMEM, VMEM, pl.ANY))
    return pl.pallas_call(
        functools.partial(attend_kernel, per_dev, kv_width // HD),
        out_shape=(
            jax.ShapeDtypeStruct((tokens, q_width), jnp.bfloat16),
            jax.ShapeDtypeStruct((tokens, LANES), jnp.float32),
            jax.ShapeDtypeStruct((2, ctx_dev, kv_width), jnp.bfloat16),
        ),
        in_specs=[smem, smem, smem, hbm, hbm, vmem, vmem, vmem, vmem],
        out_specs=(vmem, vmem, hbm),
        scratch_shapes=[
            VMEM((per_dev,) + pool_codes.shape[1:], jnp.bfloat16),
            VMEM((2, ctx_dev, kv_width), jnp.bfloat16),
            SMEM((shards,), jnp.int32),
            pltpu.SemaphoreType.DMA((per_dev,)),
            pltpu.SemaphoreType.DMA((per_dev // per_chunk, 2)),
        ],
        compiler_params=pltpu.CompilerParams(vmem_limit_bytes=40 * 2**20),
        name="attend",
    )(owner, slot, scales, pool_codes, got_codes, query, recomp_kv, own_kv, positions)


def body(
    question_hidden,
    recomp_hidden,
    norm_gain,
    w_query,
    w_keyval,
    pool_codes,
    pool_scales,
    block_owner,
    block_slot,
    recomp_pos,
):
    shards = lax.axis_size("ctx")
    q_rows = question_hidden.shape[0]
    r_rows = recomp_hidden.shape[0]
    row_count = q_rows + r_rows
    kv_width = w_keyval.shape[2]
    q_width = w_query.shape[1]
    heads = q_width // HD
    owner = block_owner[:, 0]
    per_dev = owner.shape[0] // shards
    capacity = max(2, 2 * per_dev // shards)

    send_codes = pick_blocks(owner, block_slot, pool_codes, shards, capacity)
    got_codes = lax.all_to_all(send_codes, "ctx", split_axis=0, concat_axis=0, tiled=True)
    scales = lax.all_gather(
        pool_scales.astype(jnp.float32).reshape(-1), "ctx", axis=0, tiled=True
    )

    normed = jnp.concatenate(
        [rms_rows(question_hidden, norm_gain), rms_rows(recomp_hidden, norm_gain)], axis=0
    )
    pieces = lax.all_to_all(normed, "ctx", split_axis=1, concat_axis=0, tiled=True)
    arranged = pieces.reshape(shards, row_count, pieces.shape[1])
    question_part = arranged[:, :q_rows, :].reshape(shards * q_rows, pieces.shape[1])
    query = lax.psum_scatter(
        jnp.dot(question_part, w_query, preferred_element_type=jnp.float32),
        "ctx",
        scatter_dimension=0,
        tiled=True,
    ).astype(jnp.bfloat16)
    kv_weight = w_keyval.reshape(w_keyval.shape[0], 2 * kv_width)
    projected = lax.psum_scatter(
        jnp.dot(pieces, kv_weight, preferred_element_type=jnp.float32),
        "ctx",
        scatter_dimension=0,
        tiled=True,
    ).astype(jnp.bfloat16)
    own_kv = projected[:q_rows]
    all_recomp = lax.all_gather(projected[q_rows:], "ctx", axis=0, tiled=True)
    every_query = lax.all_gather(query, "ctx", axis=0, tiled=True)

    sums, lse, kv_cache = attend(
        owner,
        block_slot,
        scales,
        pool_codes,
        got_codes,
        every_query,
        all_recomp,
        own_kv,
        recomp_pos.reshape(1, -1),
    )
    got_sums = lax.all_to_all(
        sums.reshape(shards, q_rows, q_width), "ctx", split_axis=0, concat_axis=0, tiled=True
    )
    got_lse = lax.all_to_all(
        lse.reshape(shards, q_rows, LANES), "ctx", split_axis=0, concat_axis=0, tiled=True
    )[:, :, :heads]
    share = jnp.exp2(got_lse - jnp.max(got_lse, axis=0))
    share = share / jnp.sum(share, axis=0)
    attended = jnp.sum(
        got_sums.reshape(shards, q_rows, heads, HD).astype(jnp.float32) * share[..., None], axis=0
    )
    return (attended.reshape(q_rows, q_width).astype(jnp.bfloat16), kv_cache)


def solution(mesh):
    placed = (
        P(("groups", "ctx"), None),
        P(("groups", "ctx"), None),
        P(),
        P("ctx", "tp"),
        P("ctx", None, "tp"),
        P(("groups", "ctx"), None, None, "tp"),
        P(("groups", "ctx"), None, "tp"),
        P("groups", None),
        P("groups"),
        P("groups"),
    )
    return jax.shard_map(
        body,
        mesh=mesh,
        in_specs=placed,
        out_specs=(P(("groups", "ctx"), "tp"), P(None, ("groups", "ctx"), "tp")),
        check_vma=False,
    )
```

time: 230 us -> 253 us (1.10)
  local copies, waits for them, and re-layouts: 66.5 us -> 8.11 us
  starting transfers between devices: 24.3 us -> 76.1 us
  blocking collectives: 26.9 us -> 68.9 us
  Pallas kernels: 0 us -> 41.8 us
  other arithmetic: 30.7 us -> 6.98 us
  waiting for transfers between devices: 44.8 us -> 25 us
  matrix products: 21 us -> 9.3 us
    all_to_all x1, starting transfers between devices: 4.84 us -> 68.4 us  [body(): lax.all_to_all(send_codes, 'ctx', split_axis=0, concat_axis=0, tiled=True)]
    unnamed x0 -> x1, blocking collectives: none -> 47.6 us
    pallas_call x0 -> x2, Pallas kernels: none -> 41.8 us  [the longest x1 26.4 us: pick_blocks(): pl.pallas_call(functools.partial(pick_kernel, per_dev), out_shape=jax.Sha...]
    reduce_scatter x2, waiting for transfers between devices: 20.8 us -> 0.01 us  [the longest x1 0.01 us: body(): lax.psum_scatter(jnp.dot(pieces, kv_weight, preferred_element_type=jnp.fl...]
    slice x8 -> x2, local copies, waits for them, and re-layouts: 14.7 us -> 0.01 us  [the longest x1 0.01 us: body(): all_recomp = lax.all_gather(projected[q_rows:], 'ctx', axis=0, tiled=True)]
    reshape x7 -> x2, local copies, waits for them, and re-layouts: 14.3 us -> 0.26 us  [body(): pool_scales.astype(jnp.float32).reshape(-1)]
    all_gather x1, blocking collectives: 19.4 us -> 5.92 us  [body(): all_recomp = lax.all_gather(projected[q_rows:], 'ctx', axis=0, tiled=True)]
    dot_general x6 -> x2, matrix products: 21 us -> 9.3 us  [the longest x1 5.79 us: body(): jnp.dot(question_part, w_query, preferred_element_type=jnp.float32)]
  transfers between devices with their start and end apart: 8 -> 5, of which waited for: 5 -> 2; matrix products, arithmetic and copies ran while one was open for 37% -> 5% of each run, Pallas kernels for 0% -> 11%
where the time goes in v1:
time: 253 us; the launch traced here: 251 us
  starting transfers between devices  76.1 us (30%)
  blocking collectives  68.9 us (27%)
  Pallas kernels  41.8 us (17%)
  waiting for transfers between devices  25 us (10%)
  between operations  14.9 us (6%)
  matrix products  9.3 us (4%)
  local copies, waits for them, and re-layouts  8.11 us (3%)
  other arithmetic  6.98 us (3%)
    all_to_all x1, starting transfers between devices, body(): lax.all_to_all(send_codes, 'ctx', split_axis=0, concat_axis=0, tiled=True)  68.4 us
    unnamed x1, blocking collectives  47.6 us
    pallas_call x1, Pallas kernels, pick_blocks(): pl.pallas_call(functools.partial(pick_kernel, per_dev), out_shape=jax.Sha...  26.4 us
    all_to_all x1, waiting for transfers between devices, body(): lax.all_to_all(normed, 'ctx', split_axis=1, concat_axis=0, tiled=True)  16.7 us
    pallas_call x1, Pallas kernels, attend(): pl.pallas_call(functools.partial(attend_kernel, per_dev, kv_width // HD),...  15.4 us
    all_to_all x1, waiting for transfers between devices, body(): lax.all_to_all(sums.reshape(shards, q_rows, q_width), 'ctx', split_axis=0...  8.23 us
    all_gather x1, blocking collectives, body(): every_query = lax.all_gather(query, 'ctx', axis=0, tiled=True)  7.74 us
    all_to_all x1, blocking collectives, body(): lax.all_to_all(lse.reshape(shards, q_rows, LANES), 'ctx', split_axis=0, c...  7.63 us
  transfers between devices with their start and end apart: 5, of which 2 were waited for; matrix products, arithmetic and copies ran while one was open for 5% of the time, Pallas kernels for 11%

profile of v1, /device:TPU:0, one launch (start us, length us, event | category | flops | bytes accessed | tf_op | source)
XLA Modules:
  0.0 251.1 jit_solution(15477820023130946866)
XLA Ops:
  7.2 0.8 convert_element_type.31
  8.0 1.5 fusion
  9.6 1.3 fusion.3
  10.8 0.3 fusion.2
  11.2 0.2 fusion.5
  11.4 0.1 pad_maximum_fusion
  11.5 1.3 copy.21
  12.7 4.2 %all-to-all-start.1 = ((bf16[96,4,2048]{2,0,1:T(8,128)(2,1)}), bf16[96,4,2048]{2,0,1:T(8,128)(2,1)S(1)}, u32[]{:S(2)}, u32[]{:S(2)}) async-start(bf16[96,4,2048]{2,0,1:T(8,128)(2,1)} %bitcast.20), calls=%async_computation.1 | async-start | bytes 3145728 | tf_op jit(solution)/shard_map/all_to_all | solution.py:270
  16.9 3.4 %copy.19 = bf16[256,8,2,256]{3,1,2,0:T(8,128)(2,1)} copy(bf16[256,8,2,256]{3,2,1,0:T(2,128)(2,1)} %bitcast.30) | data formatting | bytes 4194304
  20.3 16.7 %all-to-all-done.1 = bf16[96,4,2048]{2,0,1:T(8,128)(2,1)S(1)} async-done(((bf16[96,4,2048]{2,0,1:T(8,128)(2,1)}), bf16[96,4,2048]{2,0,1:T(8,128)(2,1)S(1)}, u32[]{:S(2)}, u32[]{:S(2)}) %all-to-all-start.1) | async-done | bytes 1572896 | tf_op jit(solution)/shard_map/all_to_all | solution.py:270
  37.0 3.5 %fusion.9 = f32[384,512]{1,0:T(8,128)} fusion(bf16[384,2048]{1,0:T(8,128)(2,1)S(1)} %bitcast.28, bf16[2048,512]{1,0:T(8,128)(2,1)} %bitcast.31), kind=kOutput, calls=%fused_computation.20 | convolution fusion | flops 805306368 | bytes 4456448 | tf_op jit(solution)/shard_map/dot_general | solution.py:281
  40.6 26.4 %pick_blocks.1 = bf16[4,16,2,64,256]{4,3,2,1,0:T(8,128)(2,1)} custom-call(s32[128]{0:T(128)} %bitcast.23, s32[128]{0:T(128)} %slot_ref.3, bf16[48,2,64,256]{3,2,1,0:T(8,128)(2,1)} %pool_ref.3), custom_call_target="tpu_custom_call" | custom-call | tf_op jit(solution)/shard_map/pick_blocks/pallas_call | solution.py:54
  67.0 68.4 %all-to-all-start = ((bf16[4,16,2,64,256]{4,3,2,1,0:T(8,128)(2,1)}), bf16[4,16,2,64,256]{4,3,2,1,0:T(8,128)(2,1)}, u32[]{:S(2)}, u32[]{:S(2)}) async-start(bf16[4,16,2,64,256]{4,3,2,1,0:T(8,128)(2,1)} %pick_blocks.1), calls=%async_computation | async-start | bytes 8388608 | tf_op jit(solution)/shard_map/all_to_all | solution.py:262
  135.4 5.8 %fusion.8 = f32[128,2048]{1,0:T(8,128)} fusion(bf16[128,2048]{1,0:T(8,128)(2,1)S(1)} %bitcast.27, bf16[2048,2048]{1,0:T(8,128)(2,1)} %param.13), kind=kOutput, calls=%fused_computation.19 | convolution fusion | flops 1073741824 | bytes 9961472 | tf_op jit(solution)/shard_map/dot_general | solution.py:274
  141.3 0.1 copy.16
  141.4 0.1 reshape.64
  141.6 0.6 dynamic-slice
  142.8 0.2 dynamic-update-slice
  143.1 47.6 %all-reduce.scale_ref = f32[768]{0:T(1024)S(1)} all-reduce(f32[768]{0:T(1024)S(1)} %dynamic-update-slice), channel_id=1, replica_groups=mesh['groups'=2,'ctx'=4,'tp'=4] {'ctx'}, use_global_device_ids=true, to_apply=%add | all-reduce | flops 768 | bytes 6144
  190.7 0.9 convert_element_type.36
  191.7 5.9 %all_gather.11.recomp_ref = bf16[256,512]{1,0:T(8,128)(2,1)S(1)} all-gather(bf16[64,512]{1,0:T(8,128)(2,1)S(1)} %slice.17), channel_id=1, replica_groups=mesh['groups'=2,'ctx'=4,'tp'=4] {'ctx'}, dimensions={0}, use_global_device_ids=true | all-gather | bytes 327680 | tf_op jit(solution)/shard_map/all_gather | solution.py:287
  197.6 1.0 convert_element_type.35
  198.6 7.7 %all_gather.10.query_ref = bf16[128,2048]{1,0:T(8,128)(2,1)} all-gather(bf16[32,2048]{1,0:T(8,128)(2,1)S(1)} %convert_element_type.35), channel_id=1, replica_groups=mesh['groups'=2,'ctx'=4,'tp'=4] {'ctx'}, dimensions={0}, use_global_device_ids=true | all-gather | bytes 655360 | tf_op jit(solution)/shard_map/all_gather | solution.py:288
  206.4 1.0 copy-done.1
  207.4 15.4 %attend.1 = (bf16[128,2048]{1,0:T(8,128)(2,1)S(1)}, f32[128,128]{1,0:T(8,128)S(1)}, bf16[2,2048,256]{2,1,0:T(8,128)(2,1)}) custom-call(s32[128]{0:T(128)S(1)} %bitcast.24, s32[128]{0:T(128)S(1)} %copy-done.4, f32[768]{0:T(1024)S(1)} %all-reduce.scale_ref, bf16[48,2,64,256]{3,2,1,0:T(8,128)(2,1)S(1)} %copy-done, ...), custom_call_target="tpu_custom_call" | custom-call | tf_op jit(solution)/shard_map/attend/pallas_call | solution.py:217
  222.8 0.8 copy-done.2
  223.6 7.6 %all_to_all.34 = f32[4,32,128]{2,1,0:T(8,128)S(1)} all-to-all(f32[4,32,128]{2,1,0:T(8,128)S(1)} %bitcast.22), channel_id=1, replica_groups=mesh['groups'=2,'ctx'=4,'tp'=4] {'ctx'}, dimensions={0} | all-to-all | bytes 131072 | tf_op jit(solution)/shard_map/all_to_all | solution.py:304
  231.2 3.5 %all-to-all-start.2 = ((bf16[4,32,2048]{2,1,0:T(8,128)(2,1)}), bf16[4,32,2048]{2,1,0:T(8,128)(2,1)S(1)}, u32[]{:S(2)}, u32[]{:S(2)}) async-start(bf16[4,32,2048]{2,1,0:T(8,128)(2,1)} %bitcast.21), calls=%async_computation.4 | async-start | bytes 1048576 | tf_op jit(solution)/shard_map/all_to_all | solution.py:301
  234.7 0.3 mul.59
  235.1 0.2 mul.60
  235.2 8.2 %all-to-all-done.2 = bf16[4,32,2048]{2,1,0:T(8,128)(2,1)S(1)} async-done(((bf16[4,32,2048]{2,1,0:T(8,128)(2,1)}), bf16[4,32,2048]{2,1,0:T(8,128)(2,1)S(1)}, u32[]{:S(2)}, u32[]{:S(2)}) %all-to-all-start.2) | async-done | bytes 524320 | tf_op jit(solution)/shard_map/all_to_all | solution.py:301
  243.5 0.8 multiply_reduce_fusion
  (34 shorter events, 0.2 us)
Async XLA Ops:
  7.2 3.7 %copy-start.6 = (bf16[64,8192]{1,0:T(8,128)(2,1)S(1)}, bf16[64,8192]{1,0:T(8,128)(2,1)}, u32[]{:S(2)}) copy-start(bf16[64,8192]{1,0:T(8,128)(2,1)} %param.11) | copy-start | bytes 3145732
  7.2 4.0 %copy-start.7 = (bf16[32,8192]{1,0:T(8,128)(2,1)S(1)}, bf16[32,8192]{1,0:T(8,128)(2,1)}, u32[]{:S(2)}) copy-start(bf16[32,8192]{1,0:T(8,128)(2,1)} %param.10) | copy-start | bytes 1572868
  12.7 24.3 %all-to-all-start.1 = ((bf16[96,4,2048]{2,0,1:T(8,128)(2,1)}), bf16[96,4,2048]{2,0,1:T(8,128)(2,1)S(1)}, u32[]{:S(2)}, u32[]{:S(2)}) async-start(bf16[96,4,2048]{2,0,1:T(8,128)(2,1)} %bitcast.20), calls=%async_computation.1 | async-start | bytes 3145728 | tf_op jit(solution)/shard_map/all_to_all | solution.py:270
  16.9 173.8 %reduce-scatter.5.cloned.1.call-start = ((), (), s32[]{:S(2)}) async-start(), calls=%async_computation.7 | async-start | bytes 983040 | tf_op jit(solution)/shard_map/reduce_scatter | solution.py:280
  67.0 139.4 %all-to-all-start = ((bf16[4,16,2,64,256]{4,3,2,1,0:T(8,128)(2,1)}), bf16[4,16,2,64,256]{4,3,2,1,0:T(8,128)(2,1)}, u32[]{:S(2)}, u32[]{:S(2)}) async-start(bf16[4,16,2,64,256]{4,3,2,1,0:T(8,128)(2,1)} %pick_blocks.1), calls=%async_computation | async-start | bytes 8388608 | tf_op jit(solution)/shard_map/all_to_all | solution.py:262
  135.4 62.2 %reduce-scatter.3.cloned.1.call-start = ((), (), s32[]{:S(2)}) async-start(), calls=%async_computation.6 | async-start | bytes 1310720 | tf_op jit(solution)/shard_map/reduce_scatter | solution.py:273
  135.4 5.9 %copy-start.8 = (bf16[48,2,2]{0,2,1:T(2,128)(2,1)S(1)}, bf16[48,2,2]{0,2,1:T(2,128)(2,1)}, u32[]{:S(2)}) copy-start(bf16[48,2,2]{0,2,1:T(2,128)(2,1)} %param.16) | copy-start | bytes 1156
  135.4 6.1 %copy-start.9 = (u32[32]{0:T(128)S(1)}, u32[32]{0:T(128)}, u32[]{:S(2)}) copy-start(u32[32]{0:T(128)} %constant.17) | copy-start | bytes 388
  135.4 70.9 %copy-start = (bf16[48,2,64,256]{3,2,1,0:T(8,128)(2,1)S(1)}, bf16[48,2,64,256]{3,2,1,0:T(8,128)(2,1)}, u32[]{:S(2)}) copy-start(bf16[48,2,64,256]{3,2,1,0:T(8,128)(2,1)} %pool_ref.3) | copy-start | bytes 9437188
  141.2 65.1 %copy-start.3 = (s32[128,1]{0,1:T(1,128)S(1)}, s32[128,1]{0,1:T(1,128)}, u32[]{:S(2)}) copy-start(s32[128,1]{0,1:T(1,128)} %param.17) | copy-start | bytes 1540
  141.2 65.1 %copy-start.4 = (s32[128]{0:T(128)S(1)}, s32[128]{0:T(128)}, u32[]{:S(2)}) copy-start(s32[128]{0:T(128)} %slot_ref.3) | copy-start | bytes 1540
  141.2 65.1 %copy-start.5 = (s32[256]{0:T(256)S(1)}, s32[256]{0:T(256)}, u32[]{:S(2)}) copy-start(s32[256]{0:T(256)} %param.19) | copy-start | bytes 3076
  206.3 1.0 copy-start.1
  222.8 0.8 copy-start.2
  231.2 12.3 %all-to-all-start.2 = ((bf16[4,32,2048]{2,1,0:T(8,128)(2,1)}), bf16[4,32,2048]{2,1,0:T(8,128)(2,1)S(1)}, u32[]{:S(2)}, u32[]{:S(2)}) async-start(bf16[4,32,2048]{2,1,0:T(8,128)(2,1)} %bitcast.21), calls=%async_computation.4 | async-start | bytes 1048576 | tf_op jit(solution)/shard_map/all_to_all | solution.py:301
Sparse Core Ops, SparseCore 0:
  40.7 24.3 reduce-scatter.4
  141.4 36.8 reduce-scatter.2

commit v2 on v1

--- a/solution.py
+++ b/solution.py
@@ -19,50 +19,6 @@
     floats = hidden.astype(jnp.float32)
     factor = lax.rsqrt(jnp.mean(floats * floats, axis=-1, keepdims=True) + norm_eps)
     return (floats * factor * norm_gain.astype(jnp.float32)).astype(jnp.bfloat16)
-
-
-def pick_kernel(per_dev, owner_ref, slot_ref, pool_ref, send_ref, sem):
-    me = lax.axis_index("ctx")
-    total_blocks = owner_ref.shape[0]
-
-    def step(b, carry):
-        count, total = carry
-        dest = b // per_dev
-        count = jnp.where(b % per_dev == 0, 0, count)
-        mine = (owner_ref[b] == me) & (dest != me)
-
-        @pl.when(mine)
-        def _():
-            pltpu.make_async_copy(
-                pool_ref.at[slot_ref[b]], send_ref.at[dest, count], sem
-            ).start()
-
-        more = jnp.where(mine, 1, 0)
-        return count + more, total + more
-
-    _, total = lax.fori_loop(0, total_blocks, step, (jnp.int32(0), jnp.int32(0)))
-
-    def drain(_, carry):
-        pltpu.make_async_copy(pool_ref.at[0], send_ref.at[0, 0], sem).wait()
-        return carry
-
-    lax.fori_loop(0, total, drain, 0)
-
-
-def pick_blocks(owner, slot, pool_codes, shards, capacity):
-    per_dev = owner.shape[0] // shards
-    return pl.pallas_call(
-        functools.partial(pick_kernel, per_dev),
-        out_shape=jax.ShapeDtypeStruct((shards, capacity) + pool_codes.shape[1:], pool_codes.dtype),
-        in_specs=[
-            pl.BlockSpec(memory_space=SMEM),
-            pl.BlockSpec(memory_space=SMEM),
-            pl.BlockSpec(memory_space=pl.ANY),
-        ],
-        out_specs=pl.BlockSpec(memory_space=pl.ANY),
-        scratch_shapes=[pltpu.SemaphoreType.DMA],
-        name="pick_blocks",
-    )(owner, slot, pool_codes)
 
 
 def attend_kernel(
@@ -78,10 +34,10 @@
     own_kv_ref,
     pos_ref,
     sums_ref,
-    lse_ref,
     cache_ref,
     raw,
     kv,
+    lse_ref,
     tally,
     in_sem,
     out_sem,
@@ -196,6 +152,12 @@
 
         lax.fori_loop(0, group // heads_step, one, 0)
 
+    rest = lse_ref[...]
+    for k in range(3):
+        term = rest.astype(jnp.bfloat16)
+        sums_ref[:, q_width + k * LANES : q_width + (k + 1) * LANES] = term
+        rest = rest - term.astype(jnp.float32)
+
     def finish(i, carry):
         for c in range(2):
             pltpu.make_async_copy(
@@ -217,15 +179,15 @@
     return pl.pallas_call(
         functools.partial(attend_kernel, per_dev, kv_width // HD),
         out_shape=(
-            jax.ShapeDtypeStruct((tokens, q_width), jnp.bfloat16),
-            jax.ShapeDtypeStruct((tokens, LANES), jnp.float32),
+            jax.ShapeDtypeStruct((tokens, q_width + 3 * LANES), jnp.bfloat16),
             jax.ShapeDtypeStruct((2, ctx_dev, kv_width), jnp.bfloat16),
         ),
         in_specs=[smem, smem, smem, hbm, hbm, vmem, vmem, vmem, vmem],
-        out_specs=(vmem, vmem, hbm),
+        out_specs=(vmem, hbm),
         scratch_shapes=[
             VMEM((per_dev,) + pool_codes.shape[1:], jnp.bfloat16),
             VMEM((2, ctx_dev, kv_width), jnp.bfloat16),
+            VMEM((tokens, LANES), jnp.float32),
             SMEM((shards,), jnp.int32),
             pltpu.SemaphoreType.DMA((per_dev,)),
             pltpu.SemaphoreType.DMA((per_dev // per_chunk, 2)),
@@ -258,11 +220,21 @@
     per_dev = owner.shape[0] // shards
     capacity = max(2, 2 * per_dev // shards)
 
-    send_codes = pick_blocks(owner, block_slot, pool_codes, shards, capacity)
+    own_index = lax.axis_index("ctx")
+    owners = owner.reshape(shards, per_dev)
+    positions = jnp.arange(per_dev)
+    earlier = positions[None, :] < positions[:, None]
+    same = owners[:, :, None] == owners[:, None, :]
+    rank = jnp.sum((same & earlier[None]).astype(jnp.int32), axis=2)
+    chosen = (owners == own_index)[:, :, None] & (
+        rank[:, :, None] == jnp.arange(capacity)[None, None, :]
+    )
+    send_slot = jnp.sum(
+        jnp.where(chosen, block_slot.reshape(shards, per_dev)[:, :, None], 0), axis=1
+    ).reshape(-1)
+    send_codes = pool_codes.at[send_slot].get(mode="promise_in_bounds")
+    send_codes = send_codes.reshape((shards, capacity) + pool_codes.shape[1:])
     got_codes = lax.all_to_all(send_codes, "ctx", split_axis=0, concat_axis=0, tiled=True)
-    scales = lax.all_gather(
-        pool_scales.astype(jnp.float32).reshape(-1), "ctx", axis=0, tiled=True
-    )
 
     normed = jnp.concatenate(
         [rms_rows(question_hidden, norm_gain), rms_rows(recomp_hidden, norm_gain)], axis=0
@@ -284,26 +256,41 @@
         tiled=True,
     ).astype(jnp.bfloat16)
     own_kv = projected[:q_rows]
-    all_recomp = lax.all_gather(projected[q_rows:], "ctx", axis=0, tiled=True)
+    extra = 16
+    scale_count = pool_scales.size
+    scale_rows = jnp.pad(
+        pool_scales.reshape(1, -1), ((0, extra - 1), (0, 2 * kv_width - scale_count))
+    )
+    shared = lax.all_gather(
+        jnp.concatenate([projected[q_rows:], scale_rows], axis=0), "ctx", axis=0, tiled=True
+    )
+    scales = (
+        shared.reshape(shards, r_rows + extra, 2 * kv_width)[:, r_rows, :scale_count]
+        .astype(jnp.float32)
+        .reshape(-1)
+    )
+    where_to = jnp.pad(
+        recomp_pos.reshape(shards, r_rows), ((0, 0), (0, extra)), constant_values=-1
+    ).reshape(1, -1)
     every_query = lax.all_gather(query, "ctx", axis=0, tiled=True)
 
-    sums, lse, kv_cache = attend(
+    sums, kv_cache = attend(
         owner,
         block_slot,
         scales,
         pool_codes,
         got_codes,
         every_query,
-        all_recomp,
+        shared,
         own_kv,
-        recomp_pos.reshape(1, -1),
-    )
-    got_sums = lax.all_to_all(
-        sums.reshape(shards, q_rows, q_width), "ctx", split_axis=0, concat_axis=0, tiled=True
-    )
-    got_lse = lax.all_to_all(
-        lse.reshape(shards, q_rows, LANES), "ctx", split_axis=0, concat_axis=0, tiled=True
-    )[:, :, :heads]
+        where_to,
+    )
+    got = lax.all_to_all(
+        sums.reshape(shards, q_rows, sums.shape[1]), "ctx", split_axis=0, concat_axis=0, tiled=True
+    )
+    terms = got[:, :, q_width:].astype(jnp.float32).reshape(shards, q_rows, 3, LANES)[..., :heads]
+    got_lse = terms[:, :, 0] + terms[:, :, 1] + terms[:, :, 2]
+    got_sums = got[:, :, :q_width]
     share = jnp.exp2(got_lse - jnp.max(got_lse, axis=0))
     share = share / jnp.sum(share, axis=0)
     attended = jnp.sum(

time: 253 us -> 159 us (0.63)
  starting transfers between devices: 76.1 us -> 9.11 us
  Pallas kernels: 41.8 us -> 16.1 us
  blocking collectives: 68.9 us -> 59 us
  local copies, waits for them, and re-layouts: 8.11 us -> 12.7 us
  waiting for transfers between devices: 25 us -> 28.8 us
    all_to_all x1, starting transfers between devices: 68.4 us -> 4.86 us  [body(): lax.all_to_all(send_codes, 'ctx', split_axis=0, concat_axis=0, tiled=True)]
    unnamed x1 -> x0, blocking collectives: 47.6 us -> none
    all_gather x1, blocking collectives: 5.92 us -> 38.9 us  [body(): lax.all_gather(jnp.concatenate([projected[q_rows:], scale_rows], axis=0),...]
    pallas_call x1 -> x0, Pallas kernels: 26.4 us -> none  [pick_blocks(): pl.pallas_call(functools.partial(pick_kernel, per_dev), out_shape=jax.Sha...]
    reduce_scatter x1, waiting for transfers between devices: 0.01 us -> 13.3 us  [body(): lax.psum_scatter(jnp.dot(pieces, kv_weight, preferred_element_type=jnp.fl...]
    all_to_all x1 -> x0, waiting for transfers between devices: 8.23 us -> none  [body(): lax.all_to_all(sums.reshape(shards, q_rows, q_width), 'ctx', split_axis=0...]
    all_to_all x1, blocking collectives: 7.63 us -> 12.3 us  [body(): lax.all_to_all(sums.reshape(shards, q_rows, sums.shape[1]), 'ctx', split_...]
    all_to_all x1 -> x0, starting transfers between devices: 3.47 us -> none  [body(): lax.all_to_all(sums.reshape(shards, q_rows, q_width), 'ctx', split_axis=0...]
  transfers between devices with their start and end apart: 5 -> 4, of which waited for: 2 -> 2; matrix products, arithmetic and copies ran while one was open for 5% -> 11% of each run, Pallas kernels for 11% -> 0%
where the time goes in v2:
time: 159 us; the launch traced here: 158 us
  blocking collectives  59 us (37%)
  waiting for transfers between devices  28.8 us (18%)
  Pallas kernels  16.1 us (10%)
  between operations  14.3 us (9%)
  local copies, waits for them, and re-layouts  12.7 us (8%)
  matrix products  9.73 us (6%)
  starting transfers between devices  9.11 us (6%)
  other arithmetic  8.25 us (5%)
    all_gather x1, blocking collectives, body(): lax.all_gather(jnp.concatenate([projected[q_rows:], scale_rows], axis=0),...  38.9 us
    pallas_call x1, Pallas kernels, attend(): pl.pallas_call(functools.partial(attend_kernel, per_dev, kv_width // HD),...  16.1 us
    all_to_all x1, waiting for transfers between devices, body(): lax.all_to_all(normed, 'ctx', split_axis=1, concat_axis=0, tiled=True)  15.4 us
    reduce_scatter x1, waiting for transfers between devices, body(): lax.psum_scatter(jnp.dot(pieces, kv_weight, preferred_element_type=jnp.fl...  13.3 us
    all_to_all x1, blocking collectives, body(): lax.all_to_all(sums.reshape(shards, q_rows, sums.shape[1]), 'ctx', split_...  12.3 us
    all_gather x1, blocking collectives, body(): every_query = lax.all_gather(query, 'ctx', axis=0, tiled=True)  7.74 us
    unnamed x21, local copies, waits for them, and re-layouts  6.31 us
    dot_general x1, matrix products, body(): jnp.dot(question_part, w_query, preferred_element_type=jnp.float32)  5.65 us
  transfers between devices with their start and end apart: 4, of which 2 were waited for; matrix products, arithmetic and copies ran while one was open for 11% of the time, Pallas kernels for 0%

profile of v2, /device:TPU:0, one launch (start us, length us, event | category | flops | bytes accessed | tf_op | source)
XLA Modules:
  0.0 157.9 jit_solution(7932394708147433021)
XLA Ops:
  7.2 0.8 convert_element_type.43
  8.0 1.5 fusion
  9.6 1.3 fusion.3
  10.8 0.3 fusion.2
  11.2 0.2 fusion.5
  11.5 1.3 copy.24
  12.7 4.2 %all-to-all-start = ((bf16[96,4,2048]{2,0,1:T(8,128)(2,1)}), bf16[96,4,2048]{2,0,1:T(8,128)(2,1)S(1)}, u32[]{:S(2)}, u32[]{:S(2)}) async-start(bf16[96,4,2048]{2,0,1:T(8,128)(2,1)} %bitcast.23), calls=%async_computation | async-start | bytes 3145728 | tf_op jit(solution)/shard_map/all_to_all | solution.py:242
  17.0 3.4 %copy.22 = bf16[256,8,2,256]{3,1,2,0:T(8,128)(2,1)} copy(bf16[256,8,2,256]{3,2,1,0:T(2,128)(2,1)} %bitcast.32) | data formatting | bytes 4194304
  20.3 0.5 broadcast.78
  20.8 0.7 reduce.7
  21.6 15.4 %all-to-all-done = bf16[96,4,2048]{2,0,1:T(8,128)(2,1)S(1)} async-done(((bf16[96,4,2048]{2,0,1:T(8,128)(2,1)}), bf16[96,4,2048]{2,0,1:T(8,128)(2,1)S(1)}, u32[]{:S(2)}, u32[]{:S(2)}) %all-to-all-start) | async-done | bytes 1572896 | tf_op jit(solution)/shard_map/all_to_all | solution.py:242
  37.0 1.2 copy-done.5
  38.3 4.1 %fusion.14 = f32[384,512]{1,0:T(8,128)} fusion(bf16[384,2048]{1,0:T(8,128)(2,1)} %bitcast.30, bf16[2048,512]{1,0:T(8,128)(2,1)} %bitcast.33), kind=kOutput, calls=%fused_computation.37 | convolution fusion | flops 805306368 | bytes 4456448 | tf_op jit(solution)/shard_map/dot_general | solution.py:253
  42.4 0.2 convert_reduce_fusion
  42.7 0.1 select_reduce_fusion
  43.0 2.8 %gather_fusion = bf16[64,2,64,256]{3,2,1,0:T(8,128)(2,1)} fusion(bf16[48,2,64,256]{3,2,1,0:T(8,128)(2,1)S(1)} %copy-done, s32[1024]{0:T(1024)S(1)} %pad_clamp_fusion), kind=kCustom, calls=%fused_computation | custom fusion | bytes 8388864 | tf_op jit(solution)/shard_map/gather | solution.py:235
  45.7 4.9 %all-to-all-start.1 = ((bf16[4,16,2,64,256]{4,3,2,1,0:T(8,128)(2,1)}), bf16[4,16,2,64,256]{4,3,2,1,0:T(8,128)(2,1)}, u32[]{:S(2)}, u32[]{:S(2)}) async-start(bf16[4,16,2,64,256]{4,3,2,1,0:T(8,128)(2,1)} %bitcast.27), calls=%async_computation.2 | async-start | bytes 8388608 | tf_op jit(solution)/shard_map/all_to_all | solution.py:237
  50.7 1.1 slice.44
  51.8 5.7 %fusion.15 = f32[128,2048]{1,0:T(8,128)} fusion(bf16[128,2048]{1,0:T(8,128)(2,1)S(1)} %bitcast.29, bf16[2048,2048]{1,0:T(8,128)(2,1)} %param.13), kind=kOutput, calls=%fused_computation.38 | convolution fusion | flops 1073741824 | bytes 9961472 | tf_op jit(solution)/shard_map/dot_general | solution.py:246
  57.6 0.1 reshape.140
  57.9 13.3 %reduce-scatter.3.cloned.1.call-done = f32[96,512]{1,0:T(8,128)} async-done(((f32[384,512]{1,0:T(8,128)}), f32[96,512]{1,0:T(8,128)}) %reduce-scatter.3.cloned.1.call-update) | async-done | bytes 196624 | tf_op jit(solution)/shard_map/reduce_scatter | solution.py:252
  71.3 0.9 convert_element_type.47
  72.2 38.9 %all_gather.6.recomp_ref = bf16[320,512]{1,0:T(8,128)(2,1)S(1)} all-gather(bf16[80,512]{1,0:T(8,128)(2,1)S(1)} %fusion.7), channel_id=1, replica_groups=mesh['groups'=2,'ctx'=4,'tp'=4] {'ctx'}, dimensions={0}, use_global_device_ids=true | all-gather | bytes 409600 | tf_op jit(solution)/shard_map/all_gather | solution.py:264
  111.3 1.0 convert_element_type.51
  112.2 7.7 %all_gather.7.query_ref = bf16[128,2048]{1,0:T(8,128)(2,1)} all-gather(bf16[32,2048]{1,0:T(8,128)(2,1)S(1)} %convert_element_type.51), channel_id=1, replica_groups=mesh['groups'=2,'ctx'=4,'tp'=4] {'ctx'}, dimensions={0}, use_global_device_ids=true | all-gather | bytes 655360 | tf_op jit(solution)/shard_map/all_gather | solution.py:275
  120.0 1.0 copy-done.1
  121.0 16.1 %attend.1 = (bf16[128,2432]{1,0:T(8,128)(2,1)S(1)}, bf16[2,2048,256]{2,1,0:T(8,128)(2,1)}) custom-call(s32[128]{0:T(128)S(1)} %bitcast.26, s32[128]{0:T(128)S(1)} %copy-done.2, f32[768]{0:T(1024)S(1)} %reshape.150.scale_ref, bf16[48,2,64,256]{3,2,1,0:T(8,128)(2,1)S(1)} %copy-done, bf16[4,16,2,64,256]{4,3,2,1,0:T(8,128)(2,1)} %all-to-all-done.1.codes_ref, ...), custom_call_target="tpu_custom_call" | custom-call | tf_op jit(solution)/shard_map/attend/pallas_call | solution.py:179
  137.1 12.3 %all_to_all.29 = bf16[4,32,2432]{2,1,0:T(8,128)(2,1)S(1)} all-to-all(bf16[4,32,2432]{2,1,0:T(8,128)(2,1)S(1)} %bitcast.25), channel_id=1, replica_groups=mesh['groups'=2,'ctx'=4,'tp'=4] {'ctx'}, dimensions={0} | all-to-all | bytes 1245184 | tf_op jit(solution)/shard_map/all_to_all | solution.py:288
  149.5 0.2 fusion.13
  149.8 0.3 mul.59
  150.1 0.2 mul.60
  150.3 0.8 multiply_reduce_fusion
  (45 shorter events, 1.1 us)
Async XLA Ops:
  7.2 3.7 %copy-start.4 = (bf16[64,8192]{1,0:T(8,128)(2,1)S(1)}, bf16[64,8192]{1,0:T(8,128)(2,1)}, u32[]{:S(2)}) copy-start(bf16[64,8192]{1,0:T(8,128)(2,1)} %param.11) | copy-start | bytes 3145732
  7.2 4.0 %copy-start.6 = (bf16[32,8192]{1,0:T(8,128)(2,1)S(1)}, bf16[32,8192]{1,0:T(8,128)(2,1)}, u32[]{:S(2)}) copy-start(bf16[32,8192]{1,0:T(8,128)(2,1)} %param.10) | copy-start | bytes 1572868
  12.7 24.3 %all-to-all-start = ((bf16[96,4,2048]{2,0,1:T(8,128)(2,1)}), bf16[96,4,2048]{2,0,1:T(8,128)(2,1)S(1)}, u32[]{:S(2)}, u32[]{:S(2)}) async-start(bf16[96,4,2048]{2,0,1:T(8,128)(2,1)} %bitcast.23), calls=%async_computation | async-start | bytes 3145728 | tf_op jit(solution)/shard_map/all_to_all | solution.py:242
  16.9 54.3 %reduce-scatter.3.cloned.1.call-start = ((), (), s32[]{:S(2)}) async-start(), calls=%async_computation.5 | async-start | bytes 983040 | tf_op jit(solution)/shard_map/reduce_scatter | solution.py:252
  17.0 3.9 %copy-start.3 = (s32[128,1]{0,1:T(1,128)S(1)}, s32[128,1]{0,1:T(1,128)}, u32[]{:S(2)}) copy-start(s32[128,1]{0,1:T(1,128)} %param.17) | copy-start | bytes 1540
  37.0 1.2 copy-start.5
  38.3 4.3 %copy-start.2 = (s32[128]{0:T(128)S(1)}, s32[128]{0:T(128)}, u32[]{:S(2)}) copy-start(s32[128]{0:T(128)} %slot_ref.1) | copy-start | bytes 1540
  38.3 4.7 %copy-start = (bf16[48,2,64,256]{3,2,1,0:T(8,128)(2,1)S(1)}, bf16[48,2,64,256]{3,2,1,0:T(8,128)(2,1)}, u32[]{:S(2)}) copy-start(bf16[48,2,64,256]{3,2,1,0:T(8,128)(2,1)} %pool_ref.1) | copy-start | bytes 9437188
  45.7 74.2 %all-to-all-start.1 = ((bf16[4,16,2,64,256]{4,3,2,1,0:T(8,128)(2,1)}), bf16[4,16,2,64,256]{4,3,2,1,0:T(8,128)(2,1)}, u32[]{:S(2)}, u32[]{:S(2)}) async-start(bf16[4,16,2,64,256]{4,3,2,1,0:T(8,128)(2,1)} %bitcast.27), calls=%async_computation.2 | async-start | bytes 8388608 | tf_op jit(solution)/shard_map/all_to_all | solution.py:237
  50.6 60.7 %reduce-scatter.5.cloned.1.call-start = ((), (), s32[]{:S(2)}) async-start(), calls=%async_computation.6 | async-start | bytes 1310720 | tf_op jit(solution)/shard_map/reduce_scatter | solution.py:245
  51.8 5.7 %copy-start.7 = (bf16[48,2,2]{0,2,1:T(2,128)(2,1)S(1)}, bf16[48,2,2]{0,2,1:T(2,128)(2,1)}, u32[]{:S(2)}) copy-start(bf16[48,2,2]{0,2,1:T(2,128)(2,1)} %param.16) | copy-start | bytes 1156
  51.8 6.0 %copy-start.8 = (s32[256]{0:T(256)S(1)}, s32[256]{0:T(256)}, u32[]{:S(2)}) copy-start(s32[256]{0:T(256)} %param.19) | copy-start | bytes 3076
  120.0 1.0 copy-start.1
Sparse Core Ops, SparseCore 0:
  42.5 28.7 reduce-scatter.2
  74.5 30.5 reduce-scatter.4

commit v3 on v2

--- a/solution.py
+++ b/solution.py
@@ -24,11 +24,28 @@
 def attend_kernel(
     per_dev,
     kv_heads,
+    shards,
     owner_ref,
     slot_ref,
     scale_ref,
     pool_ref,
-    codes_ref,
+    *refs,
+):
+    got_refs = refs[: shards - 1]
+    attend_body(
+        per_dev, kv_heads, shards, owner_ref, slot_ref, scale_ref, pool_ref, got_refs, *refs[shards - 1 :]
+    )
+
+
+def attend_body(
+    per_dev,
+    kv_heads,
+    shards,
+    owner_ref,
+    slot_ref,
+    scale_ref,
+    pool_ref,
+    got_refs,
     query_ref,
     recomp_ref,
     own_kv_ref,
@@ -43,7 +60,6 @@
     out_sem,
 ):
     me = lax.axis_index("ctx")
-    shards = codes_ref.shape[0]
     pool_dev = pool_ref.shape[0]
     block_len = pool_ref.shape[2]
     kv_width = kv_heads * HD
@@ -68,9 +84,13 @@
                 pool_ref.at[slot_ref[base + b]], raw.at[b], in_sem.at[b]
             ).start()
 
-        @pl.when(owner != me)
-        def _():
-            pltpu.make_async_copy(codes_ref.at[owner, rank], raw.at[b], in_sem.at[b]).start()
+        for shift in range(1, shards):
+
+            @pl.when(owner == lax.rem(me + shards - shift, shards))
+            def _(shift=shift):
+                pltpu.make_async_copy(
+                    got_refs[shift - 1].at[rank], raw.at[b], in_sem.at[b]
+                ).start()
 
         return carry
 
@@ -169,7 +189,7 @@
 
 
 def attend(owner, slot, scales, pool_codes, got_codes, query, recomp_kv, own_kv, positions):
-    shards = got_codes.shape[0]
+    shards = len(got_codes) + 1
     per_dev = owner.shape[0] // shards
     block_len, kv_width = pool_codes.shape[2:]
     tokens, q_width = query.shape
@@ -177,12 +197,12 @@
     per_chunk = math.gcd(8, per_dev)
     smem, vmem, hbm = (pl.BlockSpec(memory_space=m) for m in (SMEM, VMEM, pl.ANY))
     return pl.pallas_call(
-        functools.partial(attend_kernel, per_dev, kv_width // HD),
+        functools.partial(attend_kernel, per_dev, kv_width // HD, shards),
         out_shape=(
             jax.ShapeDtypeStruct((tokens, q_width + 3 * LANES), jnp.bfloat16),
             jax.ShapeDtypeStruct((2, ctx_dev, kv_width), jnp.bfloat16),
         ),
-        in_specs=[smem, smem, smem, hbm, hbm, vmem, vmem, vmem, vmem],
+        in_specs=[smem, smem, smem] + [hbm] * shards + [vmem, vmem, vmem, vmem],
         out_specs=(vmem, hbm),
         scratch_shapes=[
             VMEM((per_dev,) + pool_codes.shape[1:], jnp.bfloat16),
@@ -194,7 +214,7 @@
         ],
         compiler_params=pltpu.CompilerParams(vmem_limit_bytes=40 * 2**20),
         name="attend",
-    )(owner, slot, scales, pool_codes, got_codes, query, recomp_kv, own_kv, positions)
+    )(owner, slot, scales, pool_codes, *got_codes, query, recomp_kv, own_kv, positions)
 
 
 def body(
@@ -231,10 +251,15 @@
     )
     send_slot = jnp.sum(
         jnp.where(chosen, block_slot.reshape(shards, per_dev)[:, :, None], 0), axis=1
-    ).reshape(-1)
-    send_codes = pool_codes.at[send_slot].get(mode="promise_in_bounds")
-    send_codes = send_codes.reshape((shards, capacity) + pool_codes.shape[1:])
-    got_codes = lax.all_to_all(send_codes, "ctx", split_axis=0, concat_axis=0, tiled=True)
+    )
+    got_codes = []
+    for shift in range(1, shards):
+        wanted = lax.dynamic_index_in_dim(
+            send_slot, lax.rem(own_index + shift, shards), 0, keepdims=False
+        )
+        blocks = pool_codes.at[wanted].get(mode="promise_in_bounds")
+        pairs = [(i, (i + shift) % shards) for i in range(shards)]
+        got_codes.append(lax.ppermute(blocks, "ctx", pairs))
 
     normed = jnp.concatenate(
         [rms_rows(question_hidden, norm_gain), rms_rows(recomp_hidden, norm_gain)], axis=0

time: 159 us -> 157 us (0.987)
  starting transfers between devices: 9.11 us -> 6.06 us
  waiting for transfers between devices: 28.8 us -> 30.8 us
    all_to_all x1 -> x0, starting transfers between devices: 4.86 us -> none  [body(): lax.all_to_all(send_codes, 'ctx', split_axis=0, concat_axis=0, tiled=True)]
    unnamed x21 -> x17, local copies, waits for them, and re-layouts: 6.31 us -> 4.03 us
    gather x1 -> x3, local copies, waits for them, and re-layouts: 2.79 us -> 4.8 us  [body(): blocks = pool_codes.at[wanted].get(mode='promise_in_bounds')]
    ppermute x0 -> x3, starting transfers between devices: none -> 1.81 us  [body(): got_codes.append(lax.ppermute(blocks, 'ctx', pairs))]
  transfers between devices with their start and end apart: 4 -> 6, of which waited for: 2 -> 2; matrix products, arithmetic and copies ran while one was open for 11% -> 12% of each run, Pallas kernels for 0% -> 0%
where the time goes in v3:
time: 157 us; the launch traced here: 156 us
  blocking collectives  59.6 us (38%)
  waiting for transfers between devices  30.8 us (20%)
  Pallas kernels  16.2 us (10%)
  between operations  14.3 us (9%)
  local copies, waits for them, and re-layouts  11.3 us (7%)
  matrix products  9.23 us (6%)
  other arithmetic  8.27 us (5%)
  starting transfers between devices  6.06 us (4%)
    all_gather x1, blocking collectives, body(): lax.all_gather(jnp.concatenate([projected[q_rows:], scale_rows], axis=0),...  40 us
    all_to_all x1, waiting for transfers between devices, body(): lax.all_to_all(normed, 'ctx', split_axis=1, concat_axis=0, tiled=True)  16.7 us
    pallas_call x1, Pallas kernels, attend(): pl.pallas_call(functools.partial(attend_kernel, per_dev, kv_width // HD,...  16.2 us
    reduce_scatter x1, waiting for transfers between devices, body(): lax.psum_scatter(jnp.dot(pieces, kv_weight, preferred_element_type=jnp.fl...  14 us
    all_to_all x1, blocking collectives, body(): lax.all_to_all(sums.reshape(shards, q_rows, sums.shape[1]), 'ctx', split_...  12.3 us
    all_gather x1, blocking collectives, body(): every_query = lax.all_gather(query, 'ctx', axis=0, tiled=True)  7.29 us
    dot_general x1, matrix products, body(): jnp.dot(question_part, w_query, preferred_element_type=jnp.float32)  5.77 us
    gather x3, local copies, waits for them, and re-layouts, body(): blocks = pool_codes.at[wanted].get(mode='promise_in_bounds')  4.8 us
  transfers between devices with their start and end apart: 6, of which 2 were waited for; matrix products, arithmetic and copies ran while one was open for 12% of the time, Pallas kernels for 0%

profile of v3, /device:TPU:0, one launch (start us, length us, event | category | flops | bytes accessed | tf_op | source)
XLA Modules:
  0.0 155.7 jit_solution(3728868261087222330)
XLA Ops:
  7.2 0.8 convert_element_type.43
  8.0 1.5 fusion
  9.6 1.3 fusion.3
  10.8 0.3 fusion.2
  11.2 0.2 fusion.5
  11.5 1.3 copy.24
  12.7 4.2 %all-to-all-start = ((bf16[96,4,2048]{2,0,1:T(8,128)(2,1)}), bf16[96,4,2048]{2,0,1:T(8,128)(2,1)S(1)}, u32[]{:S(2)}, u32[]{:S(2)}) async-start(bf16[96,4,2048]{2,0,1:T(8,128)(2,1)} %bitcast.44), calls=%async_computation | async-start | bytes 3145728 | tf_op jit(solution)/shard_map/all_to_all | solution.py:267
  17.0 3.4 %copy.22 = bf16[256,8,2,256]{3,1,2,0:T(8,128)(2,1)} copy(bf16[256,8,2,256]{3,2,1,0:T(2,128)(2,1)} %bitcast.52) | data formatting | bytes 4194304
  20.3 16.7 %all-to-all-done = bf16[96,4,2048]{2,0,1:T(8,128)(2,1)S(1)} async-done(((bf16[96,4,2048]{2,0,1:T(8,128)(2,1)}), bf16[96,4,2048]{2,0,1:T(8,128)(2,1)S(1)}, u32[]{:S(2)}, u32[]{:S(2)}) %all-to-all-start) | async-done | bytes 1572896 | tf_op jit(solution)/shard_map/all_to_all | solution.py:267
  37.0 3.5 %fusion.19 = f32[384,512]{1,0:T(8,128)} fusion(bf16[384,2048]{1,0:T(8,128)(2,1)S(1)} %bitcast.50, bf16[2048,512]{1,0:T(8,128)(2,1)} %bitcast.53), kind=kOutput, calls=%fused_computation.51 | convolution fusion | flops 805306368 | bytes 4456448 | tf_op jit(solution)/shard_map/dot_general | solution.py:278
  40.6 5.8 %fusion.20 = f32[128,2048]{1,0:T(8,128)} fusion(bf16[128,2048]{1,0:T(8,128)(2,1)S(1)} %bitcast.49, bf16[2048,2048]{1,0:T(8,128)(2,1)} %param.13), kind=kOutput, calls=%fused_computation.52 | convolution fusion | flops 1073741824 | bytes 9961472 | tf_op jit(solution)/shard_map/dot_general | solution.py:271
  46.5 0.5 broadcast.131
  47.1 0.7 reduce.7
  47.8 0.2 convert_reduce_fusion
  48.1 0.1 select_reduce_fusion
  48.2 1.6 %gather_fusion = bf16[16,2,64,256]{3,2,1,0:T(8,128)(2,1)} fusion(bf16[48,2,64,256]{3,2,1,0:T(8,128)(2,1)S(1)} %copy-done, s32[1024]{0:T(1024)S(1)} %pad_clamp_fusion.2), kind=kCustom, calls=%fused_computation | custom fusion | bytes 2097216 | tf_op jit(solution)/shard_map/gather | solution.py:260
  49.9 1.6 %gather_fusion.1 = bf16[16,2,64,256]{3,2,1,0:T(8,128)(2,1)} fusion(bf16[48,2,64,256]{3,2,1,0:T(8,128)(2,1)S(1)} %copy-done, s32[1024]{0:T(1024)S(1)} %pad_clamp_fusion.1), kind=kCustom, calls=%fused_computation.1 | custom fusion | bytes 2097216 | tf_op jit(solution)/shard_map/gather | solution.py:260
  51.5 0.4 collective-permute-start.1
  51.8 1.6 %gather_fusion.2 = bf16[16,2,64,256]{3,2,1,0:T(8,128)(2,1)} fusion(bf16[48,2,64,256]{3,2,1,0:T(8,128)(2,1)S(1)} %copy-done, s32[1024]{0:T(1024)S(1)} %pad_clamp_fusion), kind=kCustom, calls=%fused_computation.2 | custom fusion | bytes 2097216 | tf_op jit(solution)/shard_map/gather | solution.py:260
  53.5 1.4 collective-permute-start.2
  55.0 0.1 reshape.190
  55.4 14.0 %reduce-scatter.3.cloned.1.call-done = f32[96,512]{1,0:T(8,128)} async-done(((f32[384,512]{1,0:T(8,128)}), f32[96,512]{1,0:T(8,128)}) %reduce-scatter.3.cloned.1.call-update) | async-done | bytes 196624 | tf_op jit(solution)/shard_map/reduce_scatter | solution.py:277
  69.4 0.9 convert_element_type.47
  70.4 40.0 %all_gather.6.refs_4_ = bf16[320,512]{1,0:T(8,128)(2,1)S(1)} all-gather(bf16[80,512]{1,0:T(8,128)(2,1)S(1)} %fusion.7), channel_id=1, replica_groups=mesh['groups'=2,'ctx'=4,'tp'=4] {'ctx'}, dimensions={0}, use_global_device_ids=true | all-gather | bytes 409600 | tf_op jit(solution)/shard_map/all_gather | solution.py:289
  110.5 1.0 convert_element_type.51
  111.5 7.3 %all_gather.7.refs_3_ = bf16[128,2048]{1,0:T(8,128)(2,1)S(1)} all-gather(bf16[32,2048]{1,0:T(8,128)(2,1)S(1)} %convert_element_type.51), channel_id=1, replica_groups=mesh['groups'=2,'ctx'=4,'tp'=4] {'ctx'}, dimensions={0}, use_global_device_ids=true | all-gather | bytes 655360 | tf_op jit(solution)/shard_map/all_gather | solution.py:300
  118.8 16.2 %attend.1 = (bf16[128,2432]{1,0:T(8,128)(2,1)S(1)}, bf16[2,2048,256]{2,1,0:T(8,128)(2,1)}) custom-call(s32[128]{0:T(128)S(1)} %bitcast.47, s32[128]{0:T(128)S(1)} %copy-done.1, f32[768]{0:T(1024)S(1)} %reshape.198.scale_ref, bf16[48,2,64,256]{3,2,1,0:T(8,128)(2,1)S(1)} %copy-done, bf16[16,2,64,256]{3,2,1,0:T(8,128)(2,1)} %collective-permute-done.refs_0_, ...), custom_call_target="tpu_custom_call" | custom-call | tf_op jit(solution)/shard_map/attend/pallas_call | solution.py:199
  135.0 12.3 %all_to_all.24 = bf16[4,32,2432]{2,1,0:T(8,128)(2,1)S(1)} all-to-all(bf16[4,32,2432]{2,1,0:T(8,128)(2,1)S(1)} %bitcast.46), channel_id=1, replica_groups=mesh['groups'=2,'ctx'=4,'tp'=4] {'ctx'}, dimensions={0} | all-to-all | bytes 1245184 | tf_op jit(solution)/shard_map/all_to_all | solution.py:313
  147.4 0.2 fusion.18
  147.6 0.3 mul.59
  148.0 0.2 mul.60
  148.1 0.8 multiply_reduce_fusion
  (48 shorter events, 1.1 us)
Async XLA Ops:
  7.2 3.7 %copy-start.3 = (bf16[64,8192]{1,0:T(8,128)(2,1)S(1)}, bf16[64,8192]{1,0:T(8,128)(2,1)}, u32[]{:S(2)}) copy-start(bf16[64,8192]{1,0:T(8,128)(2,1)} %param.11) | copy-start | bytes 3145732
  7.2 4.0 %copy-start.4 = (bf16[32,8192]{1,0:T(8,128)(2,1)S(1)}, bf16[32,8192]{1,0:T(8,128)(2,1)}, u32[]{:S(2)}) copy-start(bf16[32,8192]{1,0:T(8,128)(2,1)} %param.10) | copy-start | bytes 1572868
  12.7 24.3 %all-to-all-start = ((bf16[96,4,2048]{2,0,1:T(8,128)(2,1)}), bf16[96,4,2048]{2,0,1:T(8,128)(2,1)S(1)}, u32[]{:S(2)}, u32[]{:S(2)}) async-start(bf16[96,4,2048]{2,0,1:T(8,128)(2,1)} %bitcast.44), calls=%async_computation | async-start | bytes 3145728 | tf_op jit(solution)/shard_map/all_to_all | solution.py:267
  16.9 52.4 %reduce-scatter.3.cloned.1.call-start = ((), (), s32[]{:S(2)}) async-start(), calls=%async_computation.4 | async-start | bytes 983040 | tf_op jit(solution)/shard_map/reduce_scatter | solution.py:277
  40.5 70.0 %reduce-scatter.5.cloned.1.call-start = ((), (), s32[]{:S(2)}) async-start(), calls=%async_computation.5 | async-start | bytes 1310720 | tf_op jit(solution)/shard_map/reduce_scatter | solution.py:270
  40.6 5.9 %copy-start.1 = (s32[128]{0:T(128)S(1)}, s32[128]{0:T(128)}, u32[]{:S(2)}) copy-start(s32[128]{0:T(128)} %slot_ref.1) | copy-start | bytes 1540
  40.6 6.4 %copy-start.2 = (s32[128,1]{0,1:T(1,128)S(1)}, s32[128,1]{0,1:T(1,128)}, u32[]{:S(2)}) copy-start(s32[128,1]{0,1:T(1,128)} %param.17) | copy-start | bytes 1540
  40.6 7.6 %copy-start = (bf16[48,2,64,256]{3,2,1,0:T(8,128)(2,1)S(1)}, bf16[48,2,64,256]{3,2,1,0:T(8,128)(2,1)}, u32[]{:S(2)}) copy-start(bf16[48,2,64,256]{3,2,1,0:T(8,128)(2,1)} %pool_ref.1) | copy-start | bytes 9437188
  49.8 68.9 %collective-permute-start = (bf16[16,2,64,256]{3,2,1,0:T(8,128)(2,1)}, bf16[16,2,64,256]{3,2,1,0:T(8,128)(2,1)}, u32[]{:S(2)}, u32[]{:S(2)}) collective-permute-start(bf16[16,2,64,256]{3,2,1,0:T(8,128)(2,1)} %gather_fusion), channel_id=1, source_target_pairs={{0,4},{4,8},{8,12},{12,0},{1,5},{5,9},{9,13},{13,1},{2,6},{6,10},{... | collective-permute-start | bytes 3145736 | tf_op jit(solution)/shard_map/ppermute | solution.py:262
  49.8 5.1 %copy-start.5 = (bf16[48,2,2]{0,2,1:T(2,128)(2,1)S(1)}, bf16[48,2,2]{0,2,1:T(2,128)(2,1)}, u32[]{:S(2)}) copy-start(bf16[48,2,2]{0,2,1:T(2,128)(2,1)} %param.16) | copy-start | bytes 1156
  49.9 5.3 %copy-start.6 = (s32[256]{0:T(256)S(1)}, s32[256]{0:T(256)}, u32[]{:S(2)}) copy-start(s32[256]{0:T(256)} %param.19) | copy-start | bytes 3076
  51.5 67.3 %collective-permute-start.1 = (bf16[16,2,64,256]{3,2,1,0:T(8,128)(2,1)}, bf16[16,2,64,256]{3,2,1,0:T(8,128)(2,1)}, u32[]{:S(2)}, u32[]{:S(2)}) collective-permute-start(bf16[16,2,64,256]{3,2,1,0:T(8,128)(2,1)} %gather_fusion.1), channel_id=1, source_target_pairs={{0,8},{4,12},{8,0},{12,4},{1,9},{5,13},{9,1},{13,5},{2,10},{6,14},... | collective-permute-start | bytes 3145736 | tf_op jit(solution)/shard_map/ppermute | solution.py:262
  53.5 65.3 %collective-permute-start.2 = (bf16[16,2,64,256]{3,2,1,0:T(8,128)(2,1)}, bf16[16,2,64,256]{3,2,1,0:T(8,128)(2,1)}, u32[]{:S(2)}, u32[]{:S(2)}) collective-permute-start(bf16[16,2,64,256]{3,2,1,0:T(8,128)(2,1)} %gather_fusion.2), channel_id=1, source_target_pairs={{0,12},{4,0},{8,4},{12,8},{1,13},{5,1},{9,5},{13,9},{2,14},{6,2},{... | collective-permute-start | bytes 3145736 | tf_op jit(solution)/shard_map/ppermute | solution.py:262
Sparse Core Ops, SparseCore 0:
  40.6 28.6 reduce-scatter.2
  72.1 30.6 reduce-scatter.4

commit v4 on v3

--- a/solution.py
+++ b/solution.py
@@ -252,14 +252,19 @@
     send_slot = jnp.sum(
         jnp.where(chosen, block_slot.reshape(shards, per_dev)[:, :, None], 0), axis=1
     )
-    got_codes = []
+    picked = []
     for shift in range(1, shards):
         wanted = lax.dynamic_index_in_dim(
             send_slot, lax.rem(own_index + shift, shards), 0, keepdims=False
         )
-        blocks = pool_codes.at[wanted].get(mode="promise_in_bounds")
+        picked.append(pool_codes.at[wanted].get(mode="promise_in_bounds"))
+    picked, question_hidden, recomp_hidden = lax.optimization_barrier(
+        (picked, question_hidden, recomp_hidden)
+    )
+    got_codes = []
+    for shift in range(1, shards):
         pairs = [(i, (i + shift) % shards) for i in range(shards)]
-        got_codes.append(lax.ppermute(blocks, "ctx", pairs))
+        got_codes.append(lax.ppermute(picked[shift - 1], "ctx", pairs))
 
     normed = jnp.concatenate(
         [rms_rows(question_hidden, norm_gain), rms_rows(recomp_hidden, norm_gain)], axis=0

time: 157 us -> 167 us (1.064)
  waiting for transfers between devices: 30.8 us -> 37.7 us
  local copies, waits for them, and re-layouts: 11.3 us -> 16.9 us
  blocking collectives: 59.6 us -> 56.7 us
    reduce_scatter x1, waiting for transfers between devices: 14 us -> 20.3 us  [body(): lax.psum_scatter(jnp.dot(pieces, kv_weight, preferred_element_type=jnp.fl...]
    gather x3, local copies, waits for them, and re-layouts: 4.8 us -> 8.75 us  [body(): picked.append(pool_codes.at[wanted].get(mode='promise_in_bounds'))]
    all_gather x1, blocking collectives: 40 us -> 37.1 us  [body(): lax.all_gather(jnp.concatenate([projected[q_rows:], scale_rows], axis=0),...]
  transfers between devices with their start and end apart: 6 -> 6, of which waited for: 2 -> 2; matrix products, arithmetic and copies ran while one was open for 12% -> 8% of each run, Pallas kernels for 0% -> 0%
where the time goes in v4:
time: 167 us
  blocking collectives  56.7 us (34%)
  waiting for transfers between devices  37.7 us (23%)
  local copies, waits for them, and re-layouts  16.9 us (10%)
  Pallas kernels  16.1 us (10%)
  between operations  14.3 us (9%)
  matrix products  9.59 us (6%)
  other arithmetic  9.21 us (6%)
  starting transfers between devices  6.23 us (4%)
    all_gather x1, blocking collectives, body(): lax.all_gather(jnp.concatenate([projected[q_rows:], scale_rows], axis=0),...  37.1 us
    reduce_scatter x1, waiting for transfers between devices, body(): lax.psum_scatter(jnp.dot(pieces, kv_weight, preferred_element_type=jnp.fl...  20.3 us
    all_to_all x1, waiting for transfers between devices, body(): lax.all_to_all(normed, 'ctx', split_axis=1, concat_axis=0, tiled=True)  17.4 us
    pallas_call x1, Pallas kernels, attend(): pl.pallas_call(functools.partial(attend_kernel, per_dev, kv_width // HD,...  16.1 us
    all_to_all x1, blocking collectives, body(): lax.all_to_all(sums.reshape(shards, q_rows, sums.shape[1]), 'ctx', split_...  12.3 us
    gather x3, local copies, waits for them, and re-layouts, body(): picked.append(pool_codes.at[wanted].get(mode='promise_in_bounds'))  8.75 us
    all_gather x1, blocking collectives, body(): every_query = lax.all_gather(query, 'ctx', axis=0, tiled=True)  7.29 us
    dot_general x1, matrix products, body(): jnp.dot(question_part, w_query, preferred_element_type=jnp.float32)  5.65 us
  transfers between devices with their start and end apart: 6, of which 2 were waited for; matrix products, arithmetic and copies ran while one was open for 8% of the time, Pallas kernels for 0%

profile of v4, /device:TPU:0, one launch (start us, length us, event | category | flops | bytes accessed | tf_op | source)
XLA Modules:
  0.0 166.7 jit_solution(3514927151305309331)
XLA Ops:
  7.2 0.5 broadcast.131
  7.7 1.3 reduce.7
  9.1 0.2 convert_reduce_fusion
  9.3 0.7 broadcast_in_dim.14
  10.1 0.1 select_reduce_fusion
  10.3 3.6 %gather_fusion.1 = bf16[16,2,64,256]{3,2,1,0:T(8,128)(2,1)} fusion(bf16[48,2,64,256]{3,2,1,0:T(8,128)(2,1)} %pool_ref.1, s32[1024]{0:T(1024)S(1)} %get-tuple-element.22), kind=kCustom, calls=%fused_computation.1 | custom fusion | bytes 2097216 | tf_op jit(solution)/shard_map/gather | solution.py:260
  13.9 3.5 %gather_fusion.2 = bf16[16,2,64,256]{3,2,1,0:T(8,128)(2,1)} fusion(bf16[48,2,64,256]{3,2,1,0:T(8,128)(2,1)} %pool_ref.1, s32[1024]{0:T(1024)S(1)} %get-tuple-element.21), kind=kCustom, calls=%fused_computation.2 | custom fusion | bytes 2097216 | tf_op jit(solution)/shard_map/gather | solution.py:260
  17.4 1.6 gather_fusion
  19.0 1.3 fusion.3
  20.4 1.5 fusion
  22.0 1.2 fusion.5
  23.2 0.3 fusion.2
  23.6 1.2 copy.24
  24.9 4.3 %all-to-all-start = ((bf16[96,4,2048]{2,0,1:T(8,128)(2,1)}), bf16[96,4,2048]{2,0,1:T(8,128)(2,1)}, u32[]{:S(2)}, u32[]{:S(2)}) async-start(bf16[96,4,2048]{2,0,1:T(8,128)(2,1)} %bitcast.48), calls=%async_computation | async-start | bytes 3145728 | tf_op jit(solution)/shard_map/all_to_all | solution.py:272
  29.3 3.4 %copy.22 = bf16[256,8,2,256]{3,1,2,0:T(8,128)(2,1)} copy(bf16[256,8,2,256]{3,2,1,0:T(2,128)(2,1)} %bitcast.51) | data formatting | bytes 4194304
  32.6 17.4 %all-to-all-done = bf16[96,4,2048]{2,0,1:T(8,128)(2,1)} async-done(((bf16[96,4,2048]{2,0,1:T(8,128)(2,1)}), bf16[96,4,2048]{2,0,1:T(8,128)(2,1)}, u32[]{:S(2)}, u32[]{:S(2)}) %all-to-all-start) | async-done | bytes 1572896 | tf_op jit(solution)/shard_map/all_to_all | solution.py:272
  50.0 3.9 %fusion.19 = f32[384,512]{1,0:T(8,128)} fusion(bf16[384,2048]{1,0:T(8,128)(2,1)} %bitcast.8, bf16[2048,512]{1,0:T(8,128)(2,1)} %bitcast.52), kind=kOutput, calls=%fused_computation.51 | convolution fusion | flops 805306368 | bytes 4456448 | tf_op jit(solution)/shard_map/dot_general | solution.py:283
  54.0 1.1 slice.48
  55.1 5.7 %fusion.20 = f32[128,2048]{1,0:T(8,128)} fusion(bf16[128,2048]{1,0:T(8,128)(2,1)S(1)} %bitcast.50, bf16[2048,2048]{1,0:T(8,128)(2,1)} %param.13), kind=kOutput, calls=%fused_computation.52 | convolution fusion | flops 1073741824 | bytes 9961472 | tf_op jit(solution)/shard_map/dot_general | solution.py:276
  61.0 1.7 %collective-permute-start.2 = (bf16[16,2,64,256]{3,2,1,0:T(8,128)(2,1)}, bf16[16,2,64,256]{3,2,1,0:T(8,128)(2,1)}, u32[]{:S(2)}, u32[]{:S(2)}) collective-permute-start(bf16[16,2,64,256]{3,2,1,0:T(8,128)(2,1)} %gather_fusion.2), channel_id=1, source_target_pairs={{0,12},{4,0},{8,4},{12,8},{1,13},{5,1},{9,5},{13,9},{2,14},{6,2},{... | collective-permute-start | bytes 3145736 | tf_op jit(solution)/shard_map/ppermute | solution.py:267
  62.8 0.1 reshape.190
  63.1 20.3 %reduce-scatter.3.cloned.1.call-done = f32[96,512]{1,0:T(8,128)} async-done(((f32[384,512]{1,0:T(8,128)}), f32[96,512]{1,0:T(8,128)}) %reduce-scatter.3.cloned.1.call-update) | async-done | bytes 196624 | tf_op jit(solution)/shard_map/reduce_scatter | solution.py:282
  83.4 0.9 convert_element_type.48
  84.4 37.1 %all_gather.6.refs_4_ = bf16[320,512]{1,0:T(8,128)(2,1)S(1)} all-gather(bf16[80,512]{1,0:T(8,128)(2,1)S(1)} %fusion.7), channel_id=1, replica_groups=mesh['groups'=2,'ctx'=4,'tp'=4] {'ctx'}, dimensions={0}, use_global_device_ids=true | all-gather | bytes 409600 | tf_op jit(solution)/shard_map/all_gather | solution.py:294
  121.5 1.0 convert_element_type.51
  122.5 7.3 %all_gather.7.refs_3_ = bf16[128,2048]{1,0:T(8,128)(2,1)S(1)} all-gather(bf16[32,2048]{1,0:T(8,128)(2,1)S(1)} %convert_element_type.51), channel_id=1, replica_groups=mesh['groups'=2,'ctx'=4,'tp'=4] {'ctx'}, dimensions={0}, use_global_device_ids=true | all-gather | bytes 655360 | tf_op jit(solution)/shard_map/all_gather | solution.py:305
  129.8 16.1 %attend.1 = (bf16[128,2432]{1,0:T(8,128)(2,1)S(1)}, bf16[2,2048,256]{2,1,0:T(8,128)(2,1)}) custom-call(s32[128]{0:T(128)S(1)} %bitcast.47, s32[128]{0:T(128)S(1)} %copy-done.1, f32[768]{0:T(1024)S(1)} %reshape.198.scale_ref, bf16[48,2,64,256]{3,2,1,0:T(8,128)(2,1)S(1)} %copy-done, bf16[16,2,64,256]{3,2,1,0:T(8,128)(2,1)} %collective-permute-done.refs_0_, ...), custom_call_target="tpu_custom_call" | custom-call | tf_op jit(solution)/shard_map/attend/pallas_call | solution.py:199
  145.9 12.3 %all_to_all.24 = bf16[4,32,2432]{2,1,0:T(8,128)(2,1)S(1)} all-to-all(bf16[4,32,2432]{2,1,0:T(8,128)(2,1)S(1)} %bitcast.46), channel_id=1, replica_groups=mesh['groups'=2,'ctx'=4,'tp'=4] {'ctx'}, dimensions={0} | all-to-all | bytes 1245184 | tf_op jit(solution)/shard_map/all_to_all | solution.py:318
  158.3 0.2 fusion.18
  158.6 0.3 mul.59
  158.9 0.2 mul.60
  159.1 0.8 multiply_reduce_fusion
  (47 shorter events, 1.1 us)
Async XLA Ops:
  10.3 7.1 %copy-start = (bf16[48,2,64,256]{3,2,1,0:T(8,128)(2,1)S(1)}, bf16[48,2,64,256]{3,2,1,0:T(8,128)(2,1)}, u32[]{:S(2)}) copy-start(bf16[48,2,64,256]{3,2,1,0:T(8,128)(2,1)} %pool_ref.1) | copy-start | bytes 9437188
  13.9 6.5 %copy-start.4 = (bf16[8192]{0:T(1024)(128)(2,1)S(1)}, bf16[8192]{0:T(1024)(128)(2,1)}, u32[]{:S(2)}) copy-start(bf16[8192]{0:T(1024)(128)(2,1)} %param.12) | copy-start | bytes 49156
  19.0 4.2 %copy-start.3 = (bf16[64,8192]{1,0:T(8,128)(2,1)S(1)}, bf16[64,8192]{1,0:T(8,128)(2,1)}, u32[]{:S(2)}) copy-start(bf16[64,8192]{1,0:T(8,128)(2,1)} %param.11) | copy-start | bytes 3145732
  24.9 25.1 %all-to-all-start = ((bf16[96,4,2048]{2,0,1:T(8,128)(2,1)}), bf16[96,4,2048]{2,0,1:T(8,128)(2,1)}, u32[]{:S(2)}, u32[]{:S(2)}) async-start(bf16[96,4,2048]{2,0,1:T(8,128)(2,1)} %bitcast.48), calls=%async_computation | async-start | bytes 3145728 | tf_op jit(solution)/shard_map/all_to_all | solution.py:272
  29.2 54.1 %reduce-scatter.3.cloned.1.call-start = ((), (), s32[]{:S(2)}) async-start(), calls=%async_computation.4 | async-start | bytes 983040 | tf_op jit(solution)/shard_map/reduce_scatter | solution.py:282
  54.0 67.6 %reduce-scatter.5.cloned.1.call-start = ((), (), s32[]{:S(2)}) async-start(), calls=%async_computation.5 | async-start | bytes 1310720 | tf_op jit(solution)/shard_map/reduce_scatter | solution.py:275
  55.1 7.5 %copy-start.5 = (bf16[48,2,2]{0,2,1:T(2,128)(2,1)S(1)}, bf16[48,2,2]{0,2,1:T(2,128)(2,1)}, u32[]{:S(2)}) copy-start(bf16[48,2,2]{0,2,1:T(2,128)(2,1)} %param.16) | copy-start | bytes 1156
  55.1 7.8 %copy-start.6 = (s32[256]{0:T(256)S(1)}, s32[256]{0:T(256)}, u32[]{:S(2)}) copy-start(s32[256]{0:T(256)} %param.19) | copy-start | bytes 3076
  60.8 69.0 %copy-start.1 = (s32[128]{0:T(128)S(1)}, s32[128]{0:T(128)}, u32[]{:S(2)}) copy-start(s32[128]{0:T(128)} %slot_ref.1) | copy-start | bytes 1540
  60.8 69.0 %copy-start.2 = (s32[128,1]{0,1:T(1,128)S(1)}, s32[128,1]{0,1:T(1,128)}, u32[]{:S(2)}) copy-start(s32[128,1]{0,1:T(1,128)} %param.17) | copy-start | bytes 1540
  60.8 69.0 %collective-permute-start = (bf16[16,2,64,256]{3,2,1,0:T(8,128)(2,1)}, bf16[16,2,64,256]{3,2,1,0:T(8,128)(2,1)}, u32[]{:S(2)}, u32[]{:S(2)}) collective-permute-start(bf16[16,2,64,256]{3,2,1,0:T(8,128)(2,1)} %gather_fusion), channel_id=1, source_target_pairs={{0,4},{4,8},{8,12},{12,0},{1,5},{5,9},{9,13},{13,1},{2,6},{6,10},{... | collective-permute-start | bytes 3145736 | tf_op jit(solution)/shard_map/ppermute | solution.py:267
  60.9 68.9 %collective-permute-start.1 = (bf16[16,2,64,256]{3,2,1,0:T(8,128)(2,1)}, bf16[16,2,64,256]{3,2,1,0:T(8,128)(2,1)}, u32[]{:S(2)}, u32[]{:S(2)}) collective-permute-start(bf16[16,2,64,256]{3,2,1,0:T(8,128)(2,1)} %gather_fusion.1), channel_id=1, source_target_pairs={{0,8},{4,12},{8,0},{12,4},{1,9},{5,13},{9,1},{13,5},{2,10},{6,14},... | collective-permute-start | bytes 3145736 | tf_op jit(solution)/shard_map/ppermute | solution.py:267
  61.0 68.9 %collective-permute-start.2 = (bf16[16,2,64,256]{3,2,1,0:T(8,128)(2,1)}, bf16[16,2,64,256]{3,2,1,0:T(8,128)(2,1)}, u32[]{:S(2)}, u32[]{:S(2)}) collective-permute-start(bf16[16,2,64,256]{3,2,1,0:T(8,128)(2,1)} %gather_fusion.2), channel_id=1, source_target_pairs={{0,12},{4,0},{8,4},{12,8},{1,13},{5,1},{9,5},{13,9},{2,14},{6,2},{... | collective-permute-start | bytes 3145736 | tf_op jit(solution)/shard_map/ppermute | solution.py:267
Sparse Core Ops, SparseCore 0:
  54.1 29.2 reduce-scatter.2
  86.6 30.6 reduce-scatter.4
